TPU v7x, 32 devices: a whole 2x2x4 slice. The times are simulated.
32 devices in a mesh: dp: 4 (over y, core), ctx: 8 (over z, x).
Axes of the slice: x: 2, y: 2, z: 4, core: 2. Of those that a mesh axis runs over, the one named last changes fastest.
Arguments:
- mixer_input: bfloat16 [4096, 2560], P(('dp', 'ctx')), parts along dimension 0, may hold values from -6 to 6
- input_map: bfloat16 [4096, 128], P(('dp', 'ctx')), parts along dimension 0, may hold values from -6 to 6
- output_map: bfloat16 [4096, 128], P(('dp', 'ctx')), parts along dimension 0, may hold values from -0.03125 to 0.03125
- log_decay: float32 [4096, 40], P(('dp', 'ctx')), parts along dimension 0, may hold values from -1 to 0
- query_rows: bfloat16 [4096, 2560], P(('dp', 'ctx')), parts along dimension 0, may hold values from -7 to 7
- key_rows: bfloat16 [4096, 320], P(('dp', 'ctx')), parts along dimension 0, may hold values from -7 to 7
- value_rows: bfloat16 [4096, 320], P(('dp', 'ctx')), parts along dimension 0, may hold values from -6 to 6
Outputs:
- mixer_output: bfloat16 [4096, 2560], P(('dp', 'ctx')), parts along dimension 0
- attention_output: bfloat16 [4096, 2560], P(('dp', 'ctx')), parts along dimension 0
There are 4 independent parts, one for each index of `dp`. A program takes and returns all parts, laid end to end along the dimension named above; each array names one. Nothing has to cross between parts.
All inputs are finite; a program needn't handle non-finite values.
Results may differ from a plain program's by a relative error of at most 0.0049.
Values may be sent and summed in bfloat16 or wider, within the bound.
A program may use at most 128 MiB of HBM per device.

v0:
```python
import math

import jax
import jax.numpy as jnp
from jax import lax
from jax.sharding import PartitionSpec as P

MIXER_HEADS = 40
P_SIZE = 64
N = 128
QH = 32
KVH = 4
DH = 80
STRETCH = 128


masked_score = -1e30


def entering_2(part, axis, combine, identity):
    place = lax.axis_index(axis)
    gathered = jax.tree.map(lambda a: lax.all_gather(a, axis), part)
    state = jax.tree.map(lambda a, e: jnp.zeros_like(a) + jnp.asarray(e, a.dtype), part, identity)

    def one(step, state):
        return combine(
            state, jax.tree.map(lambda a: lax.dynamic_index_in_dim(a, step, 0, False), gathered)
        )

    return lax.fori_loop(0, place, one, state)


def mixer_part(mixer_input, input_map, output_map, log_decay):
    row_count = mixer_input.shape[0]
    count = row_count // STRETCH
    x_blocks = mixer_input.reshape(count, STRETCH, MIXER_HEADS, P_SIZE)
    in_blocks = input_map.reshape(count, STRETCH, N)
    out_blocks = output_map.reshape(count, STRETCH, N)
    cumulative = jnp.cumsum(log_decay.reshape(count, STRETCH, MIXER_HEADS), axis=1).transpose(
        0, 2, 1
    )
    lower_mask = jnp.tril(jnp.ones((STRETCH, STRETCH), dtype=bool))
    match = jnp.einsum("ktn,ksn->kts", out_blocks, in_blocks, preferred_element_type=jnp.float32)
    decay_gap = jnp.where(lower_mask, cumulative[..., :, None] - cumulative[..., None, :], 0.0)
    weights = jnp.where(lower_mask, match[:, None] * jnp.exp(decay_gap), 0.0).astype(jnp.bfloat16)
    inner = jnp.einsum("khts,kshp->kthp", weights, x_blocks, preferred_element_type=jnp.float32)
    tail_decay = jnp.exp(cumulative[..., -1:] - cumulative)
    weighted = (tail_decay[..., None] * in_blocks[:, None].astype(jnp.float32)).astype(jnp.bfloat16)
    updates = jnp.einsum("khsn,kshp->khnp", weighted, x_blocks, preferred_element_type=jnp.float32)
    factors = jnp.exp(cumulative[..., -1])
    zero_state = jnp.zeros((MIXER_HEADS, N, P_SIZE), jnp.float32)

    def fold_block(state, items):
        factor, update = items
        return (factor[:, None, None] * state + update, None)

    local_end, unused = lax.scan(fold_block, zero_state, (factors, updates))
    span_decay = jnp.prod(factors, axis=0)

    def combine(earlier, later):
        return (earlier[0] * later[0], later[0][:, None, None] * earlier[1] + later[1])

    prefix = entering_2(
        (span_decay, local_end),
        "ctx",
        combine,
        (jnp.ones_like(span_decay), jnp.zeros_like(local_end)),
    )
    incoming = prefix[1]

    def enter_block(state, items):
        factor, update = items
        return (factor[:, None, None] * state + update, state)

    unused_end, entering = lax.scan(enter_block, incoming, (factors, updates))
    carried = jnp.einsum(
        "ktn,khnp->kthp", out_blocks.astype(jnp.float32), entering, precision=lax.Precision.HIGHEST
    )
    carried = carried * jnp.exp(cumulative).transpose(0, 2, 1)[..., None]
    return (inner + carried).astype(jnp.bfloat16).reshape(row_count, MIXER_HEADS * P_SIZE)


def attend(query_local, key_local, value_local):
    length = query_local.shape[0]
    heads_here = query_local.shape[1] // DH
    block = min(512, length)
    block_count = length // block
    query_heads = query_local.reshape(length, heads_here, DH)
    key_heads = key_local.reshape(length, heads_here, DH)
    value_heads = value_local.reshape(length, heads_here, DH)
    scale = 1.0 / math.sqrt(DH)
    offsets = jnp.arange(block, dtype=jnp.int32)

    def one_block(query_index, result):
        query_block = lax.dynamic_slice_in_dim(query_heads, query_index * block, block, 0)

        def visit(key_index, running):
            running_max, running_sum, total = running
            key_block = lax.dynamic_slice_in_dim(key_heads, key_index * block, block, 0)
            scores = (
                jnp.einsum(
                    "thd,shd->hts", query_block, key_block, preferred_element_type=jnp.float32
                )
                * scale
            )
            visible = (key_index * block + offsets)[None, :] <= (query_index * block + offsets)[
                :, None
            ]
            scores = jnp.where(visible[None], scores, masked_score)
            new_max = jnp.maximum(running_max, jnp.max(scores, axis=-1))
            rescale = jnp.exp(running_max - new_max)
            expo = jnp.exp(scores - new_max[..., None])
            running_sum = running_sum * rescale + jnp.sum(expo, axis=-1)
            value_block = lax.dynamic_slice_in_dim(value_heads, key_index * block, block, 0)
            total = total * rescale.T[..., None] + jnp.einsum(
                "hts,shd->thd",
                expo.astype(jnp.bfloat16),
                value_block,
                preferred_element_type=jnp.float32,
            )
            return (new_max, running_sum, total)

        start = (
            jnp.full((heads_here, block), masked_score, jnp.float32),
            jnp.zeros((heads_here, block), jnp.float32),
            jnp.zeros((block, heads_here, DH), jnp.float32),
        )
        row_max, row_sum, total = lax.fori_loop(0, query_index + 1, visit, start)
        finished = (
            (total / row_sum.T[..., None]).astype(jnp.bfloat16).reshape(block, heads_here * DH)
        )
        return lax.dynamic_update_slice_in_dim(result, finished, query_index * block, 0)

    return lax.fori_loop(
        0, block_count, one_block, jnp.zeros((length, heads_here * DH), jnp.bfloat16)
    )


def attention_part(query_rows, key_rows, value_rows):
    group = QH // KVH
    heads_here = QH // lax.axis_size("ctx")
    query_local = lax.all_to_all(query_rows, "ctx", split_axis=1, concat_axis=0, tiled=True)
    key_whole, value_whole = (
        lax.all_gather(key_rows, "ctx", axis=0, tiled=True),
        lax.all_gather(value_rows, "ctx", axis=0, tiled=True),
    )
    kv_head = lax.axis_index("ctx") * heads_here // group
    key_local = jnp.tile(lax.dynamic_slice_in_dim(key_whole, kv_head * DH, DH, 1), (1, heads_here))
    value_local = jnp.tile(
        lax.dynamic_slice_in_dim(value_whole, kv_head * DH, DH, 1), (1, heads_here)
    )
    attended = attend(query_local, key_local, value_local)
    return lax.all_to_all(attended, "ctx", split_axis=0, concat_axis=1, tiled=True)


def per_device(mixer_input, input_map, output_map, log_decay, query_rows, key_rows, value_rows):
    mixer_output = mixer_part(mixer_input, input_map, output_map, log_decay)
    attention_output = attention_part(query_rows, key_rows, value_rows)
    return (mixer_output, attention_output)


def solution(mesh):
    return jax.shard_map(
        per_device,
        mesh=mesh,
        in_specs=(
            P(("dp", "ctx"), None),
            P(("dp", "ctx"), None),
            P(("dp", "ctx"), None),
            P(("dp", "ctx"), None),
            P(("dp", "ctx"), None),
            P(("dp", "ctx"), None),
            P(("dp", "ctx"), None),
        ),
        out_specs=(P(("dp", "ctx"), None), P(("dp", "ctx"), None)),
        check_vma=False,
    )
```

profile of v0, /device:TPU:26, one launch (start us, length us, event | category | flops | bytes accessed | tf_op | source)
XLA Modules:
  0.0 273.3 jit_solution(10538333398920973618)
XLA Ops:
  7.2 2.2 copy.57
  9.4 6.0 %all-to-all-start = ((bf16[128,8,320]{0,2,1:T(8,128)(2,1)}), bf16[128,8,320]{0,2,1:T(8,128)(2,1)S(1)}, u32[]{:S(2)}, u32[]{:S(2)}) async-start(bf16[128,8,320]{0,2,1:T(8,128)(2,1)} %bitcast.19), calls=%async_computation | async-start | bytes 1310720 | tf_op jit(solution)/shard_map/all_to_all | solution.py:142
  15.5 0.1 copy.49
  15.6 0.2 reduce_window_sum.11
  15.8 0.3 copy.52
  16.2 2.1 convolution_add_fusion
  18.4 45.4 %all_gather.16 = bf16[1024,320]{0,1:T(8,128)(2,1)S(1)} all-gather(bf16[128,320]{0,1:T(8,128)(2,1)S(1)} %copy-done.5), channel_id=1, replica_groups=mesh['dp'=4,'ctx'=8] {'ctx'}, dimensions={0}, use_global_device_ids=true | all-gather | bytes 737280 | tf_op jit(solution)/shard_map/all_gather | solution.py:144
  63.8 37.2 %all_gather.17 = bf16[1024,320]{0,1:T(8,128)(2,1)S(1)} all-gather(bf16[128,320]{0,1:T(8,128)(2,1)S(1)} %copy-done.6), channel_id=1, replica_groups=mesh['dp'=4,'ctx'=8] {'ctx'}, dimensions={0}, use_global_device_ids=true | all-gather | bytes 737280 | tf_op jit(solution)/shard_map/all_gather | solution.py:145
  101.0 0.7 constant_dynamic-slice_fusion.2
  101.7 0.4 copy.58
  102.1 0.3 reshape.162
  102.4 0.9 broadcast_in_dim.61
  103.3 14.8 %while.73 = (s32[]{:T(128)}, bf16[1024,320]{0,1:T(8,128)(2,1)}, bf16[1024,4,80]{0,2,1:T(8,128)(2,1)S(1)}, bf16[1024,80]{0,1:T(8,128)(2,1)S(1)}, bf16[1024,80]{0,...) while((s32[]{:T(128)}, bf16[1024,320]{0,1:T(8,128)(2,1)}, ...), condition=%wide.region_8.9_spmd.clone.clone, body=%wide.region_3.8_spmd.clone.clone.sunk | while | flops 348003328 | bytes 20681240 | solution.py:134
  103.4 1.0 reshape_tile.19
  104.6 3.6 %while.74 = (s32[]{:T(128)}, f32[4,512]{1,0:T(4,128)S(1)}, f32[4,512]{1,0:T(4,128)S(1)}, f32[512,4,80]{0,2,1:T(8,128)S(1)}, s32[]{:T(128)}, /*index=5*/s32[512]{...) while((s32[]{:T(128)}, f32[4,512]{1,0:T(4,128)S(1)}, ...), condition=%wide.region_7.7_spmd.clone, body=%wide.region_4.6_spmd.clone.sunk | while | flops 347675648 | bytes 16066763 | solution.py:128
  104.6 0.2 broadcast_compare_fusion.2
  104.8 1.0 fusion.57
  105.8 0.9 fusion.59
  106.8 1.4 fusion.60
  108.2 0.8 constant_dynamic-update-slice_fusion.2
  109.1 1.0 reshape_tile.19
  110.2 7.1 %while.74 = (s32[]{:T(128)}, f32[4,512]{1,0:T(4,128)S(1)}, f32[4,512]{1,0:T(4,128)S(1)}, f32[512,4,80]{0,2,1:T(8,128)S(1)}, s32[]{:T(128)}, /*index=5*/s32[512]{...) while((s32[]{:T(128)}, f32[4,512]{1,0:T(4,128)S(1)}, ...), condition=%wide.region_7.7_spmd.clone, body=%wide.region_4.6_spmd.clone.sunk | while | flops 347675648 | bytes 16066763 | solution.py:128
  110.2 0.2 broadcast_compare_fusion.2
  110.4 1.0 fusion.57
  111.4 0.9 fusion.59
  112.4 1.4 fusion.60
  113.8 0.2 broadcast_compare_fusion.2
  114.0 1.0 fusion.57
  115.0 0.9 fusion.59
  116.0 1.4 fusion.60
  117.4 0.8 constant_dynamic-update-slice_fusion.2
  118.2 2.1 copy_bitcast_fusion
  120.2 7.2 %all-to-all-start.1 = ((bf16[8,128,320]{1,2,0:T(8,128)(2,1)}), bf16[8,128,320]{1,2,0:T(8,128)(2,1)S(1)}, u32[]{:S(2)}, u32[]{:S(2)}) async-start(bf16[8,128,320]{1,2,0:T(8,128)(2,1)} %copy_bitcast_fusion), calls=%async_computation.1 | async-start | bytes 1310720 | tf_op jit(solution)/shard_map/all_to_all | solution.py:153
  127.5 0.1 copy.50
  127.6 39.8 %all-gather = f32[8,40,1]{1,2,0:T(1,128)S(1)} all-gather(f32[1,40,1]{1,2,0:T(1,128)S(1)} %get-tuple-element.446), channel_id=2, replica_groups=mesh['dp'=4,'ctx'=8] {'ctx'}, dimensions={0}, use_global_device_ids=true | all-gather | bytes 1440 | tf_op jit(solution)/shard_map/all_gather | solution.py:22
  167.4 0.1 fusion.39
  167.6 1.1 copy.61
  168.7 32.9 %all-gather.4.cloned.1.call-done = f32[320,128,64]{1,2,0:T(8,128)} async-done(((f32[40,128,64]{1,2,0:T(8,128)}), f32[320,128,64]{1,2,0:T(8,128)}) %all-gather.4.cloned.1.call-update) | async-done | bytes 10485776 | tf_op jit(solution)/shard_map/all_gather | solution.py:22
  201.5 1.9 broadcast.118
  203.4 56.6 %while.71 = (s32[]{:T(128)}, f32[40,128,64]{2,1,0:T(8,128)}, s32[]{:T(128)}, f32[8,40]{1,0:T(8,128)S(1)}, f32[8,40,128,64]{2,3,1,0:T(8,128)}, /*index=5*/s32[]{:T(128)}, s32[]{:T(128)}, s32[]{:T(128)}) while((s32[]{:T(128)}, f32[40,128,64]{2,1,0:T(8,128)}, s32[]{:T(128)}, f32[8,40]{1,0:T(8,128)S(1)}, f32[8,40,128,64]{2,3,1,0:T(8,128)}, ...), condition=%wide.region_2.3_spmd, body=%wide.region_1.2_spmd.sunk | while | flops 655365 | bytes 9175655 | solution.py:30
  203.4 2.5 constant_dynamic-slice_fusion.6
  205.9 1.9 copy.68
  207.9 3.6 %bitcast_add_fusion.2 = f32[40,128,64]{2,1,0:T(8,128)} fusion(f32[1,40,128,64]{3,2,1,0:T(8,128)S(1)} %copy.68, f32[40,128,64]{2,1,0:T(8,128)} %get-tuple-element.660, f32[40]{0:T(128)S(1)} %dynamic-slice_bitcast_fusion.2), kind=kLoop, calls=%fused_computation.3.clone.1 | loop fusion | flops 655360 | bytes 3932320 | tf_op jit(solution)/shard_map/while/body/add | solution.py:61
  211.5 2.5 constant_dynamic-slice_fusion.6
  214.0 1.9 copy.68
  215.9 3.6 %bitcast_add_fusion.2 = f32[40,128,64]{2,1,0:T(8,128)} fusion(f32[1,40,128,64]{3,2,1,0:T(8,128)S(1)} %copy.68, f32[40,128,64]{2,1,0:T(8,128)} %get-tuple-element.660, f32[40]{0:T(128)S(1)} %dynamic-slice_bitcast_fusion.2), kind=kLoop, calls=%fused_computation.3.clone.1 | loop fusion | flops 655360 | bytes 3932320 | tf_op jit(solution)/shard_map/while/body/add | solution.py:61
  219.6 2.5 constant_dynamic-slice_fusion.6
  222.1 1.9 copy.68
  224.0 3.6 %bitcast_add_fusion.2 = f32[40,128,64]{2,1,0:T(8,128)} fusion(f32[1,40,128,64]{3,2,1,0:T(8,128)S(1)} %copy.68, f32[40,128,64]{2,1,0:T(8,128)} %get-tuple-element.660, f32[40]{0:T(128)S(1)} %dynamic-slice_bitcast_fusion.2), kind=kLoop, calls=%fused_computation.3.clone.1 | loop fusion | flops 655360 | bytes 3932320 | tf_op jit(solution)/shard_map/while/body/add | solution.py:61
  227.6 2.5 constant_dynamic-slice_fusion.6
  230.2 1.9 copy.68
  232.1 3.6 %bitcast_add_fusion.2 = f32[40,128,64]{2,1,0:T(8,128)} fusion(f32[1,40,128,64]{3,2,1,0:T(8,128)S(1)} %copy.68, f32[40,128,64]{2,1,0:T(8,128)} %get-tuple-element.660, f32[40]{0:T(128)S(1)} %dynamic-slice_bitcast_fusion.2), kind=kLoop, calls=%fused_computation.3.clone.1 | loop fusion | flops 655360 | bytes 3932320 | tf_op jit(solution)/shard_map/while/body/add | solution.py:61
  235.7 2.5 constant_dynamic-slice_fusion.6
  238.2 1.9 copy.68
  240.2 3.6 %bitcast_add_fusion.2 = f32[40,128,64]{2,1,0:T(8,128)} fusion(f32[1,40,128,64]{3,2,1,0:T(8,128)S(1)} %copy.68, f32[40,128,64]{2,1,0:T(8,128)} %get-tuple-element.660, f32[40]{0:T(128)S(1)} %dynamic-slice_bitcast_fusion.2), kind=kLoop, calls=%fused_computation.3.clone.1 | loop fusion | flops 655360 | bytes 3932320 | tf_op jit(solution)/shard_map/while/body/add | solution.py:61
  243.8 2.5 constant_dynamic-slice_fusion.6
  246.3 1.9 copy.68
  248.3 3.6 %bitcast_add_fusion.2 = f32[40,128,64]{2,1,0:T(8,128)} fusion(f32[1,40,128,64]{3,2,1,0:T(8,128)S(1)} %copy.68, f32[40,128,64]{2,1,0:T(8,128)} %get-tuple-element.660, f32[40]{0:T(128)S(1)} %dynamic-slice_bitcast_fusion.2), kind=kLoop, calls=%fused_computation.3.clone.1 | loop fusion | flops 655360 | bytes 3932320 | tf_op jit(solution)/shard_map/while/body/add | solution.py:61
  251.9 2.5 constant_dynamic-slice_fusion.6
  254.4 1.9 copy.68
  256.4 3.6 %bitcast_add_fusion.2 = f32[40,128,64]{2,1,0:T(8,128)} fusion(f32[1,40,128,64]{3,2,1,0:T(8,128)S(1)} %copy.68, f32[40,128,64]{2,1,0:T(8,128)} %get-tuple-element.660, f32[40]{0:T(128)S(1)} %dynamic-slice_bitcast_fusion.2), kind=kLoop, calls=%fused_computation.3.clone.1 | loop fusion | flops 655360 | bytes 3932320 | tf_op jit(solution)/shard_map/while/body/add | solution.py:61
  260.0 4.0 %fusion.27 = f32[1,128,40,64]{1,3,2,0:T(8,128)S(1)} fusion(f32[40,128,64]{2,1,0:T(8,128)} %get-tuple-element.308, f32[128,40]{0,1:T(8,128)S(1)} %copy.56, bf16[128,128]{1,0:T(8,128)(2,1)S(1)} %copy-done), kind=kOutput, calls=%fused_computation.37 | convolution fusion | flops 503644160 | bytes 2674688 | tf_op jit(solution)/shard_map/ktn,khnp->kthp/dot_general | solution.py:76
  264.0 1.3 fusion.29
  265.3 1.1 copy.60
  (62 shorter events, 0.9 us)
Async XLA Ops:
  7.2 160.3 %copy-start = (bf16[128,128]{1,0:T(8,128)(2,1)S(1)}, bf16[128,128]{1,0:T(8,128)(2,1)}, u32[]{:S(2)}) copy-start(bf16[128,128]{1,0:T(8,128)(2,1)} %param.15) | copy-start | bytes 98308
  7.2 8.3 %copy-start.7 = (f32[128,40]{0,1:T(8,128)S(1)}, f32[128,40]{0,1:T(8,128)}, u32[]{:S(2)}) copy-start(f32[128,40]{0,1:T(8,128)} %param.16) | copy-start | bytes 61444
  7.2 8.6 %copy-start.3 = (bf16[128,2560]{1,0:T(8,128)(2,1)S(1)}, bf16[128,2560]{1,0:T(8,128)(2,1)}, u32[]{:S(2)}) copy-start(bf16[128,2560]{1,0:T(8,128)(2,1)} %param.13) | copy-start | bytes 1966084
  7.2 8.9 %copy-start.4 = (bf16[128,128]{1,0:T(8,128)(2,1)S(1)}, bf16[128,128]{1,0:T(8,128)(2,1)}, u32[]{:S(2)}) copy-start(bf16[128,128]{1,0:T(8,128)(2,1)} %param.14) | copy-start | bytes 98308
  9.4 92.2 %all-to-all-start = ((bf16[128,8,320]{0,2,1:T(8,128)(2,1)}), bf16[128,8,320]{0,2,1:T(8,128)(2,1)S(1)}, u32[]{:S(2)}, u32[]{:S(2)}) async-start(bf16[128,8,320]{0,2,1:T(8,128)(2,1)} %bitcast.19), calls=%async_computation | async-start | bytes 1310720 | tf_op jit(solution)/shard_map/all_to_all | solution.py:142
  15.4 186.1 %all-gather.4.cloned.1.call-start = ((), (), s32[]{:S(2)}) async-start(), calls=%async_computation.2 | async-start | bytes 11796480 | tf_op jit(solution)/shard_map/all_gather | solution.py:22
  15.4 2.9 %copy-start.5 = (bf16[128,320]{0,1:T(8,128)(2,1)S(1)}, bf16[128,320]{0,1:T(8,128)(2,1)}, u32[]{:S(2)}) copy-start(bf16[128,320]{0,1:T(8,128)(2,1)} %param.18) | copy-start | bytes 245764
  16.1 2.2 copy-start.1
  16.1 47.6 %copy-start.6 = (bf16[128,320]{0,1:T(8,128)(2,1)S(1)}, bf16[128,320]{0,1:T(8,128)(2,1)}, u32[]{:S(2)}) copy-start(bf16[128,320]{0,1:T(8,128)(2,1)} %param.19) | copy-start | bytes 245764
  120.2 47.3 %all-to-all-start.1 = ((bf16[8,128,320]{1,2,0:T(8,128)(2,1)}), bf16[8,128,320]{1,2,0:T(8,128)(2,1)S(1)}, u32[]{:S(2)}, u32[]{:S(2)}) async-start(bf16[8,128,320]{1,2,0:T(8,128)(2,1)} %copy_bitcast_fusion), calls=%async_computation.1 | async-start | bytes 1310720 | tf_op jit(solution)/shard_map/all_to_all | solution.py:153
  260.0 4.0 %copy-start.2 = (bf16[128,2560]{0,1:T(8,128)(2,1)S(1)}, bf16[128,2560]{0,1:T(8,128)(2,1)}, u32[]{:S(2)}) copy-start(bf16[128,2560]{0,1:T(8,128)(2,1)} %copy-done.1) | copy-start | bytes 1966084
Sparse Core Ops, SparseCore 0:
  18.5 183.0 all-gather.3
where the time goes:
time: 274 us; the launch traced here: 273 us
  blocking collectives  122 us (45%)
  local copies, waits for them, and re-layouts  46.4 us (17%)
  waiting for transfers between devices  32.9 us (12%)
  other arithmetic  29.1 us (11%)
  matrix products  14.6 us (5%)
  between operations  14.2 us (5%)
  starting transfers between devices  13.2 us (5%)
    all_gather x1, blocking collectives, attention_part(): lax.all_gather(key_rows, 'ctx', axis=0, tiled=True)  45.4 us
    all_gather x1, blocking collectives, entering_2(): gathered = jax.tree.map(lambda a: lax.all_gather(a, axis), part)  39.8 us
    all_gather x1, blocking collectives, attention_part(): lax.all_gather(value_rows, 'ctx', axis=0, tiled=True)  37.2 us
    all_gather x1, waiting for transfers between devices, entering_2(): gathered = jax.tree.map(lambda a: lax.all_gather(a, axis), part)  32.9 us
    dynamic_slice x14, local copies, waits for them, and re-layouts, one(): lax.dynamic_index_in_dim(a, step, 0, False)  31.1 us
    add x7, other arithmetic, combine(): later[0][:, None, None] * earlier[1] + later[1]  25.3 us
    all_to_all x1, starting transfers between devices, attention_part(): lax.all_to_all(attended, 'ctx', split_axis=0, concat_axis=1, tiled=True)  7.22 us
    all_to_all x1, starting transfers between devices, attention_part(): lax.all_to_all(query_rows, 'ctx', split_axis=1, concat_axis=0, tiled=True)  6 us
  transfers between devices with their start and end apart: 3, of which 1 were waited for; matrix products, arithmetic and copies ran while one was open for 8% of the time, Pallas kernels for 0%

commit v1 on v0

v1 whole, which is shorter than its diff:
```python
import functools
import math

import jax
import jax.numpy as jnp
from jax import lax
from jax.experimental import pallas as pl
from jax.experimental.pallas import tpu as pltpu
from jax.sharding import PartitionSpec as P

MIXER_HEADS = 40
P_SIZE = 64
N = 128
QH = 32
KVH = 4
DH = 80
T = 128
GROUP = QH // KVH
CHUNKS = 5
CW = 256
PAIRS = MIXER_HEADS // 2
SCALE = 1.0 / math.sqrt(DH)
MASKED = -1e30
MESH = pl.DeviceIdType.MESH
BF = jnp.bfloat16
F32 = jnp.float32
VMEM_LIMIT = 56 * 1024 * 1024


def iota(shape, dim):
    return lax.broadcasted_iota(jnp.int32, shape, dim)


def nt_dot(a, b):
    return lax.dot_general(a, b, (((1,), (1,)), ((), ())), preferred_element_type=F32)


def dot(a, b):
    return jnp.dot(a, b, preferred_element_type=F32)


def local_kernel(x_ref, in_ref, out_ref, ld_ref, k_ref, v_ref, u_ref, f_ref, inner_ref, ecum_ref, kv_ref):
    kv_ref[:, : KVH * DH] = k_ref[...]
    kv_ref[:, KVH * DH :] = v_ref[...]
    lower = iota((T, T), 0) >= iota((T, T), 1)
    tril = jnp.where(lower, 1.0, 0.0).astype(F32)
    cum = jnp.dot(tril, ld_ref[...], precision=lax.Precision.HIGHEST, preferred_element_type=F32)
    cum_t = jnp.concatenate([cum, jnp.zeros((T, T - MIXER_HEADS), F32)], axis=1).T
    ecum = jnp.exp(cum)
    ecum_ref[...] = ecum
    match = jnp.where(lower, nt_dot(out_ref[...], in_ref[...]), 0.0)
    in_t = in_ref[...].astype(F32).T
    left = iota((T, T), 1) < P_SIZE
    for j in range(PAIRS):
        stack = []
        tails = []
        for h in (2 * j, 2 * j + 1):
            row = cum_t[h : h + 1, :]
            gap = jnp.minimum(cum[:, h : h + 1] - row, 0.0)
            stack.append((match * jnp.exp(gap)).astype(BF))
            tails.append((in_t * jnp.exp(cum[T - 1 : T, h : h + 1] - row)).astype(BF))
        out = dot(jnp.concatenate(stack + tails, axis=0), x_ref[:, j * T : (j + 1) * T])
        inner_ref[:, j * T : (j + 1) * T] = jnp.where(left, out[:T], out[T : 2 * T])
        half, place = divmod(j, PAIRS // 2)
        c, lane = divmod(place * T, CW)
        u_ref[half, c, :, lane : lane + T] = jnp.where(left, out[2 * T : 3 * T], out[3 * T :])
        last = ecum[T - 1 : T, :]
        f_ref[half, :, place * T : (place + 1) * T] = jnp.where(
            left[:1], last[:, 2 * j : 2 * j + 1], last[:, 2 * j + 1 : 2 * j + 2]
        )


def exchange_kernel(
    n, u_ref, f_ref, kv_ref, kvall_ref, ent_ref,
    own, usend, urecv, frecv, sin, sout, entsend,
    us_sem, ur_sem, f_sem, ss_sem, sr_sem, es_sem, er_sem, kvs_sem, kvr_sem, px_sem, loc_sem,
):
    dp = lax.axis_index("dp")
    me = lax.axis_index("ctx")
    a, b = me // 2, me % 2
    rows = n // 2
    partner = (dp, a * 2 + 1 - b)

    barrier = pltpu.get_barrier_semaphore()
    pl.semaphore_signal(barrier, inc=1, device_id=partner, device_id_type=MESH)
    for d in range(1, rows):
        pl.semaphore_signal(
            barrier, inc=1, device_id=(dp, lax.rem(a + d, rows) * 2 + b), device_id_type=MESH
        )
    pl.semaphore_wait(barrier, rows)

    def ucopy(c):
        return pltpu.make_async_remote_copy(
            src_ref=usend.at[c], dst_ref=urecv.at[c], send_sem=us_sem.at[c],
            recv_sem=ur_sem.at[c], device_id=partner, device_id_type=MESH)

    def fcopy():
        return pltpu.make_async_remote_copy(
            src_ref=f_ref.at[1 - b], dst_ref=frecv, send_sem=f_sem.at[0],
            recv_sem=f_sem.at[1], device_id=partner, device_id_type=MESH)

    def scopy(c):
        return pltpu.make_async_remote_copy(
            src_ref=sout.at[c], dst_ref=sin.at[c], send_sem=ss_sem.at[c],
            recv_sem=sr_sem.at[c], device_id=(dp, (a + 1) * 2 + b), device_id_type=MESH)

    def ecopy(c):
        return pltpu.make_async_remote_copy(
            src_ref=entsend.at[c], dst_ref=ent_ref.at[b, c], send_sem=es_sem.at[c],
            recv_sem=er_sem.at[c], device_id=partner, device_id_type=MESH)

    def kvcopy(d):
        return pltpu.make_async_remote_copy(
            src_ref=own, dst_ref=kvall_ref.at[me], send_sem=kvs_sem.at[d],
            recv_sem=kvr_sem.at[me], device_id=(dp, (a + d) * 2 + b), device_id_type=MESH)

    def kvforward(d, block):
        return pltpu.make_async_remote_copy(
            src_ref=kvall_ref.at[block], dst_ref=kvall_ref.at[block], send_sem=px_sem.at[d],
            recv_sem=kvr_sem.at[block], device_id=partner, device_id_type=MESH)

    def kvarrive(block):
        return pltpu.make_async_copy(kvall_ref.at[block], kvall_ref.at[block], kvr_sem.at[block])

    fcopy().start()
    for c in range(CHUNKS):
        usend[c] = u_ref[1 - b, c].astype(BF)
        ucopy(c).start()
    own[...] = kv_ref[...]
    kvall_ref[me] = kv_ref[...]

    @pl.when(b == 0)
    def _():
        kvforward(0, me).start()
        kvall_ref[me + 1] = jnp.zeros((T, 2 * KVH * DH), BF)

    for d in range(1, rows):
        @pl.when(a + d < rows)
        def _():
            kvcopy(d).start()

    fcopy().wait_recv()
    first = b == 0
    f_own = f_ref[b]
    f_other = frecv[...]
    f_early = jnp.where(first, f_own, f_other)
    f_late = jnp.where(first, f_other, f_own)
    f_pair = f_early * f_late

    for c in range(CHUNKS):
        lanes = slice(c * CW, (c + 1) * CW)
        ucopy(c).wait_recv()
        u_own = u_ref[b, c]
        u_other = urecv[c].astype(F32)
        early = jnp.where(first, u_own, u_other)
        late = jnp.where(first, u_other, u_own)
        pair = f_late[:, lanes] * early + late

        @pl.when(a == 0)
        def _():
            sin[c] = jnp.zeros((T, CW), BF)

        @pl.when(a > 0)
        def _():
            scopy(c).wait_recv()

        state = sin[c].astype(F32)

        @pl.when(a + 1 < rows)
        def _():
            sout[c] = (f_pair[:, lanes] * state + pair).astype(BF)
            scopy(c).start()

        middle = f_early[:, lanes] * state + early
        entsend[c] = jnp.where(first, middle, state).astype(BF)
        ecopy(c).start()
        ent_ref[b, c] = jnp.where(first, state, middle).astype(BF)

        if c + 1 < rows:
            d = c + 1

            @pl.when(a - d >= 0)
            def _():
                kvarrive(me - 2 * d).wait()
                kvforward(d, me - 2 * d).start()

    for d in range(CHUNKS + 1, rows):
        @pl.when(a - d >= 0)
        def _():
            kvarrive(me - 2 * d).wait()
            kvforward(d, me - 2 * d).start()

    for d in range(rows):
        block = (a - d) * 2 + 1 - b
        valid = (a - d >= 0) if d > 0 else (b == 1)

        @pl.when(valid)
        def _():
            kvarrive(block).wait()

    for c in range(CHUNKS):
        ucopy(c).wait_send()
        ecopy(c).wait_send()
        ecopy(c).wait_recv()

        @pl.when(a + 1 < rows)
        def _():
            scopy(c).wait_send()
    fcopy().wait_send()

    @pl.when(b == 0)
    def _():
        kvforward(0, me).wait_send()

    for d in range(1, rows):
        @pl.when(a + d < rows)
        def _():
            kvcopy(d).wait_send()

        @pl.when(a - d >= 0)
        def _():
            kvforward(d, me - 2 * d).wait_send()


def attend_group(n, g, a, b, q_ref, kvall_ref, att_ref, qs, ks, vs, sc, top, total, acc):
    wide = 2 * T
    for r in range(GROUP):
        h = g * GROUP + r
        qs[r * T : (r + 1) * T, :] = q_ref[:, h * DH : (h + 1) * DH]
    kc = g * DH
    vc = (KVH + g) * DH

    def fill(p, _):
        for e in range(2):
            at = pl.ds(pl.multiple_of(p * wide + e * T, T), T)
            ks[at, :] = kvall_ref[2 * p + e, :, kc : kc + DH]
            vs[at, :] = kvall_ref[2 * p + e, :, vc : vc + DH]
        return 0

    lax.fori_loop(0, a + 1, fill, 0)
    chunk = 2 * T
    parts = GROUP * T // chunk

    def visible():
        return iota((chunk, wide), 1) <= (iota((chunk, wide), 0) % T) + b * T

    at = pl.ds(pl.multiple_of(a * wide, wide), wide)
    for r in range(parts):
        rows = slice(r * chunk, (r + 1) * chunk)
        s = nt_dot(qs[rows, :], ks[at, :]) * SCALE
        s = jnp.where(visible(), s, MASKED)
        sc[a, rows, :] = s
        top[rows, :] = jnp.maximum(s[:, :T], s[:, T:])

    def score(p, _):
        at = pl.ds(pl.multiple_of(p * wide, wide), wide)
        for r in range(parts):
            rows = slice(r * chunk, (r + 1) * chunk)
            s = nt_dot(qs[rows, :], ks[at, :]) * SCALE
            sc[p, rows, :] = s
            top[rows, :] = jnp.maximum(top[rows, :], jnp.maximum(s[:, :T], s[:, T:]))
        return 0

    lax.fori_loop(0, a, score, 0)
    for r in range(parts):
        rows = slice(r * chunk, (r + 1) * chunk)
        peak = jnp.max(top[rows, :], axis=1, keepdims=True)
        top[rows, :] = jnp.broadcast_to(peak, (chunk, T))
        total[rows, :] = jnp.zeros((chunk, T), F32)
        acc[rows, :] = jnp.zeros((chunk, DH), F32)

    def gather(p, _):
        at = pl.ds(pl.multiple_of(p * wide, wide), wide)
        for r in range(parts):
            rows = slice(r * chunk, (r + 1) * chunk)
            peak = top[rows, :]
            e0 = jnp.exp(sc[p, rows, :T] - peak)
            e1 = jnp.exp(sc[p, rows, T:] - peak)
            total[rows, :] += e0 + e1
            e = jnp.concatenate([e0.astype(BF), e1.astype(BF)], axis=1)
            acc[rows, :] += dot(e, vs[at, :])
        return 0

    lax.fori_loop(0, a + 1, gather, 0)
    outs = []
    for r in range(GROUP):
        rows = slice(r * T, (r + 1) * T)
        outs.append((acc[rows, :] / jnp.sum(total[rows, :], axis=1, keepdims=True)).astype(BF))
    wide_out = GROUP * DH
    att_ref[:, g * wide_out : (g + 1) * wide_out] = jnp.concatenate(outs, axis=1)


def finish_kernel(n, q_ref, kvall_ref, out_ref, ent_ref, inner_ref, ecum_ref, mix_ref, att_ref, *scratch):
    me = lax.axis_index("ctx")
    a, b = me // 2, me % 2
    for g in range(KVH):
        attend_group(n, g, a, b, q_ref, kvall_ref, att_ref, *scratch)
    left = iota((T, T), 1) < P_SIZE
    for half in range(2):
        for c in range(CHUNKS):
            carried = dot(out_ref[...], ent_ref[half, c])
            for e in range(CW // T):
                j = (half * CHUNKS + c) * (CW // T) + e
                factor = jnp.where(
                    left, ecum_ref[:, 2 * j : 2 * j + 1], ecum_ref[:, 2 * j + 1 : 2 * j + 2]
                )
                cols = slice(j * T, (j + 1) * T)
                mix_ref[:, cols] = (
                    inner_ref[:, cols] + carried[:, e * T : (e + 1) * T] * factor
                ).astype(BF)


def specs(count):
    return [pl.BlockSpec(memory_space=pltpu.VMEM)] * count


def per_device(n, mixer_input, input_map, output_map, log_decay, query_rows, key_rows, value_rows):
    width = MIXER_HEADS * P_SIZE
    u, f, inner, ecum, kv = pl.pallas_call(
        local_kernel,
        out_shape=(
            jax.ShapeDtypeStruct((2, CHUNKS, N, CW), F32),
            jax.ShapeDtypeStruct((2, 1, width // 2), F32),
            jax.ShapeDtypeStruct((T, width), F32),
            jax.ShapeDtypeStruct((T, MIXER_HEADS), F32),
            jax.ShapeDtypeStruct((T, 2 * KVH * DH), BF),
        ),
        in_specs=specs(6),
        out_specs=specs(5),
        compiler_params=pltpu.CompilerParams(vmem_limit_bytes=VMEM_LIMIT),
        name="local",
    )(mixer_input, input_map, output_map, log_decay, key_rows, value_rows)
    rows = n // 2
    sem = pltpu.SemaphoreType.DMA
    chunked = pltpu.VMEM((CHUNKS, N, CW), BF)
    kvall, ent = pl.pallas_call(
        functools.partial(exchange_kernel, n),
        out_shape=(
            jax.ShapeDtypeStruct((n, T, 2 * KVH * DH), BF),
            jax.ShapeDtypeStruct((2, CHUNKS, N, CW), BF),
        ),
        in_specs=specs(3),
        out_specs=specs(2),
        scratch_shapes=[
            pltpu.VMEM((T, 2 * KVH * DH), BF),
            chunked, chunked, pltpu.VMEM((1, width // 2), F32), chunked, chunked, chunked,
            sem((CHUNKS,)), sem((CHUNKS,)), sem((2,)), sem((CHUNKS,)), sem((CHUNKS,)),
            sem((CHUNKS,)), sem((CHUNKS,)), sem((rows,)), sem((n,)), sem((rows,)), sem((1,)),
        ],
        compiler_params=pltpu.CompilerParams(
            collective_id=0, has_side_effects=True, vmem_limit_bytes=VMEM_LIMIT
        ),
        name="exchange",
    )(u, f, kv)
    big = GROUP * T
    return pl.pallas_call(
        functools.partial(finish_kernel, n),
        out_shape=(
            jax.ShapeDtypeStruct((T, width), BF),
            jax.ShapeDtypeStruct((T, QH * DH), BF),
        ),
        in_specs=specs(6),
        out_specs=specs(2),
        scratch_shapes=[
            pltpu.VMEM((big, DH), BF),
            pltpu.VMEM((n * T, DH), BF),
            pltpu.VMEM((n * T, DH), BF),
            pltpu.VMEM((rows, big, 2 * T), F32),
            pltpu.VMEM((big, T), F32),
            pltpu.VMEM((big, T), F32),
            pltpu.VMEM((big, DH), F32),
        ],
        compiler_params=pltpu.CompilerParams(vmem_limit_bytes=VMEM_LIMIT),
        name="finish",
    )(query_rows, kvall, output_map, ent, inner, ecum)


def solution(mesh):
    rows = P(("dp", "ctx"), None)
    return jax.shard_map(
        functools.partial(per_device, mesh.shape["ctx"]),
        mesh=mesh,
        in_specs=(rows,) * 7,
        out_specs=(rows, rows),
        check_vma=False,
    )
```

time: 274 us -> 70.6 us (0.26)
  blocking collectives: 122 us -> 0 us
  Pallas kernels: 0 us -> 64 us
  local copies, waits for them, and re-layouts: 46.4 us -> 4.69 us
  waiting for transfers between devices: 32.9 us -> 0 us
  other arithmetic: 29.1 us -> 0 us
  matrix products: 14.6 us -> 0 us
  between operations: 14.2 us -> 0.64 us
  starting transfers between devices: 13.2 us -> 0 us
    all_gather x3 -> x0, blocking collectives: 122 us -> none  [the longest x1 45.4 us: attention_part(): lax.all_gather(key_rows, 'ctx', axis=0, tiled=True)]
    pallas_call x0 -> x3, Pallas kernels: none -> 64 us  [the longest x1 41.6 us: per_device(): pl.pallas_call(functools.partial(exchange_kernel, n), out_shape=(jax.Shap...]
    all_gather x1 -> x0, waiting for transfers between devices: 32.9 us -> none  [entering_2(): gathered = jax.tree.map(lambda a: lax.all_gather(a, axis), part)]
    dynamic_slice x18 -> x0, local copies, waits for them, and re-layouts: 31.8 us -> none  [the longest x14 31.1 us: one(): lax.dynamic_index_in_dim(a, step, 0, False)]
    add x13 -> x0, other arithmetic: 25.3 us -> none  [the longest x7 25.3 us: combine(): later[0][:, None, None] * earlier[1] + later[1]]
    dot_general x10 -> x0, matrix products: 14.6 us -> none  [the longest x3 4.07 us: visit(): jnp.einsum('hts,shd->thd', expo.astype(jnp.bfloat16), value_block, prefer...]
    all_to_all x2 -> x0, starting transfers between devices: 13.2 us -> none  [the longest x1 7.22 us: attention_part(): lax.all_to_all(attended, 'ctx', split_axis=0, concat_axis=1, tiled=True)]
    another operation x11 -> x0, local copies, waits for them, and re-layouts: 4.13 us -> none
  transfers between devices with their start and end apart: 3 -> 0, of which waited for: 1 -> 0; matrix products, arithmetic and copies ran while one was open for 8% -> 0% of each run, Pallas kernels for 0% -> 0%
where the time goes in v1:
time: 70.6 us; the launch traced here: 69.4 us
  Pallas kernels  64 us (91%)
  local copies, waits for them, and re-layouts  4.69 us (7%)
    pallas_call x1, Pallas kernels, per_device(): pl.pallas_call(functools.partial(exchange_kernel, n), out_shape=(jax.Shap...  41.6 us
    pallas_call x1, Pallas kernels, per_device(): pl.pallas_call(functools.partial(finish_kernel, n), out_shape=(jax.ShapeD...  18.3 us
    unnamed x3, local copies, waits for them, and re-layouts  4.69 us
    pallas_call x1, Pallas kernels, per_device(): pl.pallas_call(local_kernel, out_shape=(jax.ShapeDtypeStruct((2, CHUNKS,...  4.08 us

profile of v1, /device:TPU:26, one launch (start us, length us, event | category | flops | bytes accessed | tf_op | source)
XLA Modules:
  0.0 69.4 jit_solution(4249936437894562450)
XLA Ops:
  0.6 1.4 %copy.9.ld_ref = f32[128,40]{1,0:T(8,128)} copy(f32[128,40]{0,1:T(8,128)} %param.10) | data formatting | bytes 40960 | tf_op args[3]
  2.1 1.6 %copy.10.k_ref = bf16[128,320]{1,0:T(8,128)(2,1)} copy(bf16[128,320]{0,1:T(8,128)(2,1)} %param.12) | data formatting | bytes 163840 | tf_op args[5]
  3.7 1.6 %copy.11.v_ref = bf16[128,320]{1,0:T(8,128)(2,1)} copy(bf16[128,320]{0,1:T(8,128)(2,1)} %param.13) | data formatting | bytes 163840 | tf_op args[6]
  5.3 4.1 %local.1 = (f32[2,5,128,256]{3,2,1,0:T(8,128)}, f32[2,1,1280]{2,1,0:T(1,128)}, f32[128,2560]{1,0:T(8,128)}, f32[128,40]{1,0:T(8,128)}, bf16[128,640]{1,0:T(8,128)(2,1)}) custom-call(bf16[128,2560]{1,0:T(8,128)(2,1)} %x_ref.1, bf16[128,128]{1,0:T(8,128)(2,1)} %in_ref.1, bf16[128,128]{1,0:T(8,128)(2,1)} %out_ref.3, f32[128,40]{1,0:T(8,128)} %copy.9.ld_ref, ...), custom_call_target="tpu_custom_call" | custom-call | tf_op jit(solution)/shard_map/local/pallas_call | solution.py:319
  9.4 41.6 %exchange.1 = (bf16[8,128,640]{2,1,0:T(8,128)(2,1)}, bf16[2,5,128,256]{3,2,1,0:T(8,128)(2,1)}) custom-call(f32[2,5,128,256]{3,2,1,0:T(8,128)} %get-tuple-element.9.u_ref, f32[2,1,1280]{2,1,0:T(1,128)} %get-tuple-element.10.f_ref, bf16[128,640]{1,0:T(8,128)(2,1)} %get-tuple-element.11.kv_ref), custom_call_target="tpu_custom_call" | custom-call | tf_op jit(solution)/shard_map/exchange/pallas_call | solution.py:336
  51.0 18.3 %finish.1 = (bf16[128,2560]{1,0:T(8,128)(2,1)}, bf16[128,2560]{1,0:T(8,128)(2,1)}) custom-call(bf16[128,2560]{1,0:T(8,128)(2,1)} %q_ref.1, bf16[8,128,640]{2,1,0:T(8,128)(2,1)} %get-tuple-element.12.kvall_ref, bf16[128,128]{1,0:T(8,128)(2,1)} %out_ref.3, bf16[2,5,128,256]{3,2,1,0:T(8,128)(2,1)} %get-tuple-element.13.ent_ref, ...), custom_call_target="tpu_custom_call" | custom-call | tf_op jit(solution)/shard_map/finish/pallas_call | solution.py:356

commit v2 on v0

v2 whole, which is shorter than its diff:
```python
import functools
import math

import jax
import jax.numpy as jnp
from jax import lax
from jax.experimental import pallas as pl
from jax.experimental.pallas import tpu as pltpu
from jax.sharding import PartitionSpec as P

MIXER_HEADS = 40
P_SIZE = 64
N = 128
QH = 32
KVH = 4
DH = 80
T = 128
GROUP = QH // KVH
KV_ROWS = 2 * KVH * DH
CHUNKS = 5
CW = 256
PAIRS = MIXER_HEADS // 2
HALF = MIXER_HEADS * P_SIZE // 2
EXP_SCALE = math.log2(math.e) / math.sqrt(DH)
MASKED = -1e30
MESH = pl.DeviceIdType.MESH
BF = jnp.bfloat16
F32 = jnp.float32
VMEM_LIMIT = 56 * 1024 * 1024


def iota(shape, dim):
    return lax.broadcasted_iota(jnp.int32, shape, dim)


def nt_dot(a, b):
    return lax.dot_general(a, b, (((1,), (1,)), ((), ())), preferred_element_type=F32)


def dot(a, b):
    return jnp.dot(a, b, preferred_element_type=F32)


def kernel(
    n, x_ref, in_ref, out_ref, ld_ref, q_ref, k_ref, v_ref, mix_ref, att_ref,
    kvall, u, f, inner, ecum_ref, usend, urecv, frecv, sin, sout, entsend, ent,
    qs, top, total, acc,
    us_sem, ur_sem, f_sem, ss_sem, sr_sem, es_sem, er_sem, kvs_sem, kvr_sem, px_sem,
):
    dp = lax.axis_index("dp")
    me = lax.axis_index("ctx")
    a, b = me // 2, me % 2
    rows = n // 2
    partner = (dp, a * 2 + 1 - b)
    ahead = (dp, lax.rem(a + 1, rows) * 2 + b)
    behind = (dp, lax.rem(a + rows - 1, rows) * 2 + b)
    first = b == 0

    def ucopy(c):
        return pltpu.make_async_remote_copy(
            src_ref=usend.at[c], dst_ref=urecv.at[c], send_sem=us_sem.at[c],
            recv_sem=ur_sem.at[c], device_id=partner, device_id_type=MESH)

    def fcopy():
        return pltpu.make_async_remote_copy(
            src_ref=f.at[1 - b], dst_ref=frecv, send_sem=f_sem.at[0],
            recv_sem=f_sem.at[1], device_id=partner, device_id_type=MESH)

    def scopy(c):
        return pltpu.make_async_remote_copy(
            src_ref=sout.at[c], dst_ref=sin.at[c], send_sem=ss_sem.at[c],
            recv_sem=sr_sem.at[c], device_id=ahead, device_id_type=MESH)

    def ecopy(c):
        return pltpu.make_async_remote_copy(
            src_ref=entsend.at[c], dst_ref=ent.at[b, c], send_sem=es_sem.at[c],
            recv_sem=er_sem.at[c], device_id=partner, device_id_type=MESH)

    def kvhop(d):
        block = me - 2 * d
        return pltpu.make_async_remote_copy(
            src_ref=kvall.at[block], dst_ref=kvall.at[block], send_sem=kvs_sem.at[d],
            recv_sem=kvr_sem.at[block], device_id=ahead, device_id_type=MESH)

    def kvside(d):
        block = me - 2 * d
        return pltpu.make_async_remote_copy(
            src_ref=kvall.at[block], dst_ref=kvall.at[block], send_sem=px_sem.at[d],
            recv_sem=kvr_sem.at[block], device_id=partner, device_id_type=MESH)

    def kvarrive(block):
        pltpu.make_async_copy(kvall.at[block], kvall.at[block], kvr_sem.at[block]).wait()

    barrier = pltpu.get_barrier_semaphore()
    for device in (partner, ahead, behind):
        pl.semaphore_signal(barrier, inc=1, device_id=device, device_id_type=MESH)
    kvall[me, : KVH * DH, :] = k_ref[...]
    kvall[me, KVH * DH :, :] = v_ref[...]
    pl.semaphore_wait(barrier, 3)

    @pl.when(a + 1 < rows)
    def _():
        kvhop(0).start()

    lower = iota((T, T), 0) >= iota((T, T), 1)
    triu = jnp.where(iota((T, T), 0) <= iota((T, T), 1), 1.0, 0.0).astype(F32)
    cum_t = jnp.dot(ld_ref[...], triu, precision=lax.Precision.HIGHEST, preferred_element_type=F32)
    cum = jnp.concatenate([cum_t, jnp.zeros((T - MIXER_HEADS, T), F32)], axis=0).T
    ecum = jnp.exp(cum)
    ecum_ref[...] = ecum
    match = jnp.where(lower, nt_dot(out_ref[...], in_ref[...]), 0.0)
    in_t = in_ref[...].astype(F32).T
    left = iota((T, T), 1) < P_SIZE
    last = ecum[T - 1 : T, :]
    for j in range(PAIRS):
        half, place = divmod(j, PAIRS // 2)
        f[half, :, place * T : (place + 1) * T] = jnp.where(
            left[:1], last[:, 2 * j : 2 * j + 1], last[:, 2 * j + 1 : 2 * j + 2]
        )
    fcopy().start()
    for c in range(CHUNKS):
        for half in range(2):
            for e in range(CW // T):
                j = (half * CHUNKS + c) * (CW // T) + e
                stack = []
                tails = []
                for h in (2 * j, 2 * j + 1):
                    row = cum_t[h : h + 1, :]
                    gap = jnp.minimum(cum[:, h : h + 1] - row, 0.0)
                    stack.append((match * jnp.exp(gap)).astype(BF))
                    tails.append((in_t * jnp.exp(row[:, T - 1 :] - row)).astype(BF))
                cols = slice(j * T, (j + 1) * T)
                out = dot(jnp.concatenate(stack + tails, axis=0), x_ref[:, cols])
                inner[:, cols] = jnp.where(left, out[:T], out[T : 2 * T])
                u[half, c, :, e * T : (e + 1) * T] = jnp.where(
                    left, out[2 * T : 3 * T], out[3 * T :]
                )
        usend[c] = u[1 - b, c].astype(BF)
        ucopy(c).start()
        if c == 0:
            @pl.when(first)
            def _():
                kvside(0).start()

    @pl.when(first)
    def _():
        kvall[me + 1] = jnp.zeros((KV_ROWS, T), BF)

    def hand_on(d):
        @pl.when(a - d >= 0)
        def _():
            kvarrive(me - 2 * d)
            kvside(d).start()

            @pl.when(a + 1 < rows)
            def _():
                kvhop(d).start()

    def chain():
        fcopy().wait_recv()
        f_own = f[b]
        f_other = frecv[...]
        f_early = jnp.where(first, f_own, f_other)
        f_late = jnp.where(first, f_other, f_own)
        f_pair = f_early * f_late
        for c in range(CHUNKS):
            lanes = slice(c * CW, (c + 1) * CW)
            ucopy(c).wait_recv()
            u_own = u[b, c]
            u_other = urecv[c].astype(F32)
            early = jnp.where(first, u_own, u_other)
            late = jnp.where(first, u_other, u_own)
            pair = f_late[:, lanes] * early + late

            @pl.when(a == 0)
            def _():
                sin[c] = jnp.zeros((T, CW), BF)

            @pl.when(a > 0)
            def _():
                scopy(c).wait_recv()

            state = sin[c].astype(F32)

            @pl.when(a + 1 < rows)
            def _():
                sout[c] = (f_pair[:, lanes] * state + pair).astype(BF)
                scopy(c).start()

            middle = f_early[:, lanes] * state + early
            entsend[c] = jnp.where(first, middle, state).astype(BF)
            ecopy(c).start()
            ent[b, c] = jnp.where(first, state, middle).astype(BF)

    chunk = 2 * T
    parts = GROUP * T // chunk

    def attend(p, opening):
        def group(g, _):
            kc = pl.ds(pl.multiple_of(g * DH, 16), DH)
            vc = pl.ds(pl.multiple_of((KVH + g) * DH, 16), DH)
            keys = jnp.concatenate([kvall[2 * p, kc, :], kvall[2 * p + 1, kc, :]], axis=1)
            values = jnp.concatenate([kvall[2 * p, vc, :], kvall[2 * p + 1, vc, :]], axis=1)
            if opening:
                width = GROUP * DH
                q = q_ref[:, pl.ds(pl.multiple_of(g * width, T), width)]
                for r in range(GROUP):
                    qs[g, r * T : (r + 1) * T, :] = q[:, r * DH : (r + 1) * DH]
            for r in range(parts):
                at = slice(r * chunk, (r + 1) * chunk)
                s = dot(qs[g, at, :], keys)
                if opening:
                    shown = iota((chunk, chunk), 1) <= (iota((chunk, chunk), 0) % T) + b * T
                    s = jnp.where(shown, s, MASKED)
                peak = jnp.max(jnp.maximum(s[:, :T], s[:, T:]), axis=1, keepdims=True)
                if not opening:
                    old = top[g, at, :]
                    peak = jnp.maximum(old, peak)
                    shrink = jnp.exp2((old - peak) * EXP_SCALE)
                else:
                    peak = jnp.broadcast_to(peak, (chunk, T))
                top[g, at, :] = peak
                e0 = jnp.exp2((s[:, :T] - peak) * EXP_SCALE)
                e1 = jnp.exp2((s[:, T:] - peak) * EXP_SCALE)
                e = jnp.concatenate([e0.astype(BF), e1.astype(BF)], axis=1)
                summed = nt_dot(e, values)
                if opening:
                    total[g, at, :] = e0 + e1
                    acc[g, at, :] = summed
                else:
                    total[g, at, :] = total[g, at, :] * shrink + (e0 + e1)
                    acc[g, at, :] = acc[g, at, :] * shrink[:, :DH] + summed
            return 0

        lax.fori_loop(0, KVH, group, 0)

    def finish(g, _):
        width = GROUP * DH
        outs = []
        for r in range(GROUP):
            at = slice(r * T, (r + 1) * T)
            outs.append((acc[g, at, :] / jnp.sum(total[g, at, :], axis=1, keepdims=True)).astype(BF))
        att_ref[:, pl.ds(pl.multiple_of(g * width, T), width)] = jnp.concatenate(outs, axis=1)
        return 0

    chain_at = min(2, rows - 1)
    for d in range(rows):
        if d + 1 < rows:
            hand_on(d + 1)
        when = {0: a <= 1, chain_at: a > chain_at}.get(d, a == d + 1)
        if d <= chain_at:
            pl.when(when)(chain)

        @pl.when((b == 1) if d == 0 else (a - d >= 0))
        def _():
            kvarrive((a - d) * 2 + 1 - b)

        if d == 0:
            attend(a, True)
        else:
            @pl.when(a - d >= 0)
            def _():
                attend(a - d, False)

    lax.fori_loop(0, KVH, finish, 0)

    for c in range(CHUNKS):
        ecopy(c).wait_recv()
        for half in range(2):
            carried = dot(out_ref[...], ent[half, c])
            for e in range(CW // T):
                j = (half * CHUNKS + c) * (CW // T) + e
                factor = jnp.where(
                    left, ecum_ref[:, 2 * j : 2 * j + 1], ecum_ref[:, 2 * j + 1 : 2 * j + 2]
                )
                cols = slice(j * T, (j + 1) * T)
                mix_ref[:, cols] = (
                    inner[:, cols] + carried[:, e * T : (e + 1) * T] * factor
                ).astype(BF)

    fcopy().wait_send()
    for c in range(CHUNKS):
        ucopy(c).wait_send()
        ecopy(c).wait_send()

        @pl.when(a + 1 < rows)
        def _():
            scopy(c).wait_send()

    @pl.when(first)
    def _():
        kvside(0).wait_send()

    for d in range(rows):
        @pl.when((a - d >= 0) & (a + 1 < rows))
        def _():
            kvhop(d).wait_send()

        if d > 0:
            @pl.when(a - d >= 0)
            def _():
                kvside(d).wait_send()


def specs(count):
    return [pl.BlockSpec(memory_space=pltpu.VMEM)] * count


def per_device(n, mixer_input, input_map, output_map, log_decay, query_rows, key_rows, value_rows):
    width = MIXER_HEADS * P_SIZE
    rows = n // 2
    sem = pltpu.SemaphoreType.DMA
    chunked = pltpu.VMEM((CHUNKS, N, CW), BF)
    big = GROUP * T
    return pl.pallas_call(
        functools.partial(kernel, n),
        out_shape=(
            jax.ShapeDtypeStruct((T, width), BF),
            jax.ShapeDtypeStruct((T, QH * DH), BF),
        ),
        in_specs=specs(7),
        out_specs=specs(2),
        scratch_shapes=[
            pltpu.VMEM((n, KV_ROWS, T), BF),
            pltpu.VMEM((2, CHUNKS, N, CW), F32),
            pltpu.VMEM((2, 1, HALF), F32),
            pltpu.VMEM((T, width), F32),
            pltpu.VMEM((T, T), F32),
            chunked, chunked, pltpu.VMEM((1, HALF), F32), chunked, chunked, chunked,
            pltpu.VMEM((2, CHUNKS, N, CW), BF),
            pltpu.VMEM((KVH, big, DH), BF),
            pltpu.VMEM((KVH, big, T), F32),
            pltpu.VMEM((KVH, big, T), F32),
            pltpu.VMEM((KVH, big, DH), F32),
            sem((CHUNKS,)), sem((CHUNKS,)), sem((2,)), sem((CHUNKS,)), sem((CHUNKS,)),
            sem((CHUNKS,)), sem((CHUNKS,)), sem((rows,)), sem((n,)), sem((rows,)),
        ],
        compiler_params=pltpu.CompilerParams(
            collective_id=0, has_side_effects=True, vmem_limit_bytes=VMEM_LIMIT
        ),
        name="mix_and_attend",
    )(mixer_input, input_map, output_map, log_decay.T, query_rows, key_rows.T, value_rows.T)


def solution(mesh):
    rows = P(("dp", "ctx"), None)
    return jax.shard_map(
        functools.partial(per_device, mesh.shape["ctx"]),
        mesh=mesh,
        in_specs=(rows,) * 7,
        out_specs=(rows, rows),
        check_vma=False,
    )
```

time: 274 us -> 39.2 us (0.14)
  blocking collectives: 122 us -> 0 us
  local copies, waits for them, and re-layouts: 46.4 us -> 2.87 us
  Pallas kernels: 0 us -> 35.5 us
  waiting for transfers between devices: 32.9 us -> 0 us
  other arithmetic: 29.1 us -> 0 us
  matrix products: 14.6 us -> 0 us
  between operations: 14.2 us -> 0.65 us
  starting transfers between devices: 13.2 us -> 0 us
    all_gather x3 -> x0, blocking collectives: 122 us -> none  [the longest x1 45.4 us: attention_part(): lax.all_gather(key_rows, 'ctx', axis=0, tiled=True)]
    pallas_call x0 -> x1, Pallas kernels: none -> 35.5 us  [per_device(): pl.pallas_call(functools.partial(kernel, n), out_shape=(jax.ShapeDtypeStr...]
    all_gather x1 -> x0, waiting for transfers between devices: 32.9 us -> none  [entering_2(): gathered = jax.tree.map(lambda a: lax.all_gather(a, axis), part)]
    dynamic_slice x18 -> x0, local copies, waits for them, and re-layouts: 31.8 us -> none  [the longest x14 31.1 us: one(): lax.dynamic_index_in_dim(a, step, 0, False)]
    add x13 -> x0, other arithmetic: 25.3 us -> none  [the longest x7 25.3 us: combine(): later[0][:, None, None] * earlier[1] + later[1]]
    dot_general x10 -> x0, matrix products: 14.6 us -> none  [the longest x3 4.07 us: visit(): jnp.einsum('hts,shd->thd', expo.astype(jnp.bfloat16), value_block, prefer...]
    all_to_all x2 -> x0, starting transfers between devices: 13.2 us -> none  [the longest x1 7.22 us: attention_part(): lax.all_to_all(attended, 'ctx', split_axis=0, concat_axis=1, tiled=True)]
    another operation x11 -> x0, local copies, waits for them, and re-layouts: 4.13 us -> none
  transfers between devices with their start and end apart: 3 -> 0, of which waited for: 1 -> 0; matrix products, arithmetic and copies ran while one was open for 8% -> 0% of each run, Pallas kernels for 0% -> 0%
where the time goes in v2:
time: 39.2 us; the launch traced here: 39 us
  Pallas kernels  35.5 us (91%)
  local copies, waits for them, and re-layouts  2.87 us (7%)
  between operations  0.65 us (2%)
    pallas_call x1, Pallas kernels, per_device(): pl.pallas_call(functools.partial(kernel, n), out_shape=(jax.ShapeDtypeStr...  35.5 us
    unnamed x4, local copies, waits for them, and re-layouts  2.87 us

profile of v2, /device:TPU:26, one launch (start us, length us, event | category | flops | bytes accessed | tf_op | source)
XLA Modules:
  0.0 39.0 jit_solution(10905544751424184771)
XLA Ops:
  0.6 35.5 %mix_and_attend.1 = (bf16[128,2560]{1,0:T(8,128)(2,1)}, bf16[128,2560]{1,0:T(8,128)(2,1)}) custom-call(bf16[128,2560]{1,0:T(8,128)(2,1)} %x_ref.1, bf16[128,128]{1,0:T(8,128)(2,1)} %in_ref.1, bf16[128,128]{1,0:T(8,128)(2,1)} %out_ref.1, f32[40,128]{1,0:T(8,128)} %bitcast.5, bf16[128,2560]{1,0:T(8,128)(2,1)} %q_ref.1, bf16[320,128]{1,0:T(8,128)(2,1)} %bitcast.3, ...), custom_call_target="tpu_custom_call" | custom-call | tf_op jit(solution)/shard_map/mix_and_attend/pallas_call | solution.py:315
  36.1 0.0 copy-start
  36.1 2.0 %copy.11 = bf16[128,2560]{1,0:T(8,128)(2,1)} copy(bf16[128,2560]{1,0:T(8,128)(2,1)} %get-tuple-element.4) | data formatting | bytes 1310720
  38.2 0.0 copy-done
  38.2 0.8 %copy.12 = bf16[128,2560]{1,0:T(8,128)(2,1)} copy(bf16[128,2560]{1,0:T(8,128)(2,1)S(1)} %copy-done) | data formatting | bytes 1310720
Async XLA Ops:
  36.1 2.0 %copy-start = (bf16[128,2560]{1,0:T(8,128)(2,1)S(1)}, bf16[128,2560]{1,0:T(8,128)(2,1)}, u32[]{:S(2)}) copy-start(bf16[128,2560]{1,0:T(8,128)(2,1)} %get-tuple-element.5) | copy-start | bytes 1966084

commit v3 on v2

--- a/solution.py
+++ b/solution.py
@@ -192,8 +192,7 @@
             ecopy(c).start()
             ent[b, c] = jnp.where(first, state, middle).astype(BF)
 
-    chunk = 2 * T
-    parts = GROUP * T // chunk
+    wide = 2 * T
 
     def attend(p, opening):
         def group(g, _):
@@ -204,32 +203,42 @@
             if opening:
                 width = GROUP * DH
                 q = q_ref[:, pl.ds(pl.multiple_of(g * width, T), width)]
-                for r in range(GROUP):
-                    qs[g, r * T : (r + 1) * T, :] = q[:, r * DH : (r + 1) * DH]
-            for r in range(parts):
-                at = slice(r * chunk, (r + 1) * chunk)
-                s = dot(qs[g, at, :], keys)
+                queries = jnp.concatenate([q[:, r * DH : (r + 1) * DH] for r in range(GROUP)], axis=0)
+                qs[g] = queries
+                shown = iota((T, wide), 1) <= iota((T, wide), 0) + b * T
+            else:
+                queries = qs[g]
+                old_top = top[g]
+                old_total = total[g]
+                old_acc = acc[g]
+            scores = dot(queries, keys)
+            peaks, totals, shrinks, expos = [], [], [], []
+            for r in range(GROUP):
+                at = slice(r * T, (r + 1) * T)
+                s = scores[at]
                 if opening:
-                    shown = iota((chunk, chunk), 1) <= (iota((chunk, chunk), 0) % T) + b * T
                     s = jnp.where(shown, s, MASKED)
                 peak = jnp.max(jnp.maximum(s[:, :T], s[:, T:]), axis=1, keepdims=True)
-                if not opening:
-                    old = top[g, at, :]
-                    peak = jnp.maximum(old, peak)
-                    shrink = jnp.exp2((old - peak) * EXP_SCALE)
+                if opening:
+                    peak = jnp.broadcast_to(peak, (T, T))
                 else:
-                    peak = jnp.broadcast_to(peak, (chunk, T))
-                top[g, at, :] = peak
+                    peak = jnp.maximum(old_top[at], peak)
+                    shrinks.append(jnp.exp2((old_top[at] - peak) * EXP_SCALE))
+                peaks.append(peak)
                 e0 = jnp.exp2((s[:, :T] - peak) * EXP_SCALE)
                 e1 = jnp.exp2((s[:, T:] - peak) * EXP_SCALE)
-                e = jnp.concatenate([e0.astype(BF), e1.astype(BF)], axis=1)
-                summed = nt_dot(e, values)
+                totals.append(e0 + e1)
+                expos.append(jnp.concatenate([e0.astype(BF), e1.astype(BF)], axis=1))
+            summed = nt_dot(jnp.concatenate(expos, axis=0), values)
+            for r in range(GROUP):
+                at = slice(r * T, (r + 1) * T)
+                top[g, at, :] = peaks[r]
                 if opening:
-                    total[g, at, :] = e0 + e1
-                    acc[g, at, :] = summed
+                    total[g, at, :] = totals[r]
+                    acc[g, at, :] = summed[at]
                 else:
-                    total[g, at, :] = total[g, at, :] * shrink + (e0 + e1)
-                    acc[g, at, :] = acc[g, at, :] * shrink[:, :DH] + summed
+                    total[g, at, :] = old_total[at] * shrinks[r] + totals[r]
+                    acc[g, at, :] = old_acc[at] * shrinks[r][:, :DH] + summed[at]
             return 0
 
         lax.fori_loop(0, KVH, group, 0)
@@ -243,25 +252,30 @@
         att_ref[:, pl.ds(pl.multiple_of(g * width, T), width)] = jnp.concatenate(outs, axis=1)
         return 0
 
-    chain_at = min(2, rows - 1)
-    for d in range(rows):
-        if d + 1 < rows:
-            hand_on(d + 1)
-        when = {0: a <= 1, chain_at: a > chain_at}.get(d, a == d + 1)
-        if d <= chain_at:
-            pl.when(when)(chain)
-
-        @pl.when((b == 1) if d == 0 else (a - d >= 0))
+    hand_on(1)
+
+    @pl.when(a == 0)
+    def _():
+        chain()
+
+    @pl.when(b == 1)
+    def _():
+        kvarrive(me - 1)
+
+    attend(a, True)
+
+    def step(d, _):
+        hand_on(d + 1)
+
+        @pl.when(a == d)
         def _():
-            kvarrive((a - d) * 2 + 1 - b)
-
-        if d == 0:
-            attend(a, True)
-        else:
-            @pl.when(a - d >= 0)
-            def _():
-                attend(a - d, False)
-
+            chain()
+
+        kvarrive((a - d) * 2 + 1 - b)
+        attend(a - d, False)
+        return 0
+
+    lax.fori_loop(1, a + 1, step, 0)
     lax.fori_loop(0, KVH, finish, 0)
 
     for c in range(CHUNKS):

time: 39.2 us -> 39.6 us (1.010)
  the two profiles are of different devices: /device:TPU:26 before, /device:TPU:28 now
where the time goes in v3:
time: 39.6 us; the launch traced here: 39.4 us
  Pallas kernels  35.9 us (91%)
  local copies, waits for them, and re-layouts  2.87 us (7%)
  between operations  0.65 us (2%)
    pallas_call x1, Pallas kernels, per_device(): pl.pallas_call(functools.partial(kernel, n), out_shape=(jax.ShapeDtypeStr...  35.9 us
    unnamed x4, local copies, waits for them, and re-layouts  2.87 us

profile of v3, /device:TPU:28, one launch (start us, length us, event | category | flops | bytes accessed | tf_op | source)
XLA Modules:
  0.0 39.4 jit_solution(3426362059212226115)
XLA Ops:
  0.6 35.9 %mix_and_attend.1 = (bf16[128,2560]{1,0:T(8,128)(2,1)}, bf16[128,2560]{1,0:T(8,128)(2,1)}) custom-call(bf16[128,2560]{1,0:T(8,128)(2,1)} %x_ref.1, bf16[128,128]{1,0:T(8,128)(2,1)} %in_ref.1, bf16[128,128]{1,0:T(8,128)(2,1)} %out_ref.1, f32[40,128]{1,0:T(8,128)} %bitcast.5, bf16[128,2560]{1,0:T(8,128)(2,1)} %q_ref.1, bf16[320,128]{1,0:T(8,128)(2,1)} %bitcast.3, ...), custom_call_target="tpu_custom_call" | custom-call | tf_op jit(solution)/shard_map/mix_and_attend/pallas_call | solution.py:329
  36.6 0.0 copy-start
  36.6 2.0 %copy.11 = bf16[128,2560]{1,0:T(8,128)(2,1)} copy(bf16[128,2560]{1,0:T(8,128)(2,1)} %get-tuple-element.4) | data formatting | bytes 1310720
  38.6 0.0 copy-done
  38.6 0.8 %copy.12 = bf16[128,2560]{1,0:T(8,128)(2,1)} copy(bf16[128,2560]{1,0:T(8,128)(2,1)S(1)} %copy-done) | data formatting | bytes 1310720
Async XLA Ops:
  36.6 2.0 %copy-start = (bf16[128,2560]{1,0:T(8,128)(2,1)S(1)}, bf16[128,2560]{1,0:T(8,128)(2,1)}, u32[]{:S(2)}) copy-start(bf16[128,2560]{1,0:T(8,128)(2,1)} %get-tuple-element.5) | copy-start | bytes 1966084

commit v4 on v3

--- a/solution.py
+++ b/solution.py
@@ -55,6 +55,9 @@
     ahead = (dp, lax.rem(a + 1, rows) * 2 + b)
     behind = (dp, lax.rem(a + rows - 1, rows) * 2 + b)
     first = b == 0
+    crossing = rows // 2
+    early_pair = a < crossing
+    more = a + 1 < rows
 
     def ucopy(c):
         return pltpu.make_async_remote_copy(
@@ -76,10 +79,10 @@
             src_ref=entsend.at[c], dst_ref=ent.at[b, c], send_sem=es_sem.at[c],
             recv_sem=er_sem.at[c], device_id=partner, device_id_type=MESH)
 
-    def kvhop(d):
-        block = me - 2 * d
-        return pltpu.make_async_remote_copy(
-            src_ref=kvall.at[block], dst_ref=kvall.at[block], send_sem=kvs_sem.at[d],
+    def kvhop(d, e):
+        block = (a - d) * 2 + e
+        return pltpu.make_async_remote_copy(
+            src_ref=kvall.at[block], dst_ref=kvall.at[block], send_sem=kvs_sem.at[d, e],
             recv_sem=kvr_sem.at[block], device_id=ahead, device_id_type=MESH)
 
     def kvside(d):
@@ -98,9 +101,9 @@
     kvall[me, KVH * DH :, :] = v_ref[...]
     pl.semaphore_wait(barrier, 3)
 
-    @pl.when(a + 1 < rows)
-    def _():
-        kvhop(0).start()
+    @pl.when(more)
+    def _():
+        kvhop(0, b).start()
 
     lower = iota((T, T), 0) >= iota((T, T), 1)
     triu = jnp.where(iota((T, T), 0) <= iota((T, T), 1), 1.0, 0.0).astype(F32)
@@ -138,23 +141,32 @@
         usend[c] = u[1 - b, c].astype(BF)
         ucopy(c).start()
         if c == 0:
-            @pl.when(first)
+            @pl.when(first | early_pair)
             def _():
                 kvside(0).start()
 
-    @pl.when(first)
+    @pl.when(first & jnp.logical_not(early_pair))
     def _():
         kvall[me + 1] = jnp.zeros((KV_ROWS, T), BF)
 
     def hand_on(d):
-        @pl.when(a - d >= 0)
+        @pl.when(a - d >= crossing)
         def _():
             kvarrive(me - 2 * d)
             kvside(d).start()
 
-            @pl.when(a + 1 < rows)
-            def _():
-                kvhop(d).start()
+            @pl.when(more)
+            def _():
+                kvhop(d, b).start()
+
+        @pl.when((a - d >= 0) & (a - d < crossing))
+        def _():
+            for e in range(2):
+                kvarrive((a - d) * 2 + e)
+
+                @pl.when(more)
+                def _():
+                    kvhop(d, e).start()
 
     def chain():
         fcopy().wait_recv()
@@ -182,7 +194,7 @@
 
             state = sin[c].astype(F32)
 
-            @pl.when(a + 1 < rows)
+            @pl.when(more)
             def _():
                 sout[c] = (f_pair[:, lanes] * state + pair).astype(BF)
                 scopy(c).start()
@@ -258,9 +270,13 @@
     def _():
         chain()
 
-    @pl.when(b == 1)
-    def _():
-        kvarrive(me - 1)
+    @pl.when((b == 1) | early_pair)
+    def _():
+        kvarrive(a * 2 + 1 - b)
+
+    @pl.when(early_pair)
+    def _():
+        kvhop(0, 1 - b).start()
 
     attend(a, True)
 
@@ -271,7 +287,11 @@
         def _():
             chain()
 
-        kvarrive((a - d) * 2 + 1 - b)
+
+        @pl.when(a - d >= crossing)
+        def _():
+            kvarrive((a - d) * 2 + 1 - b)
+
         attend(a - d, False)
         return 0
 
@@ -297,23 +317,39 @@
         ucopy(c).wait_send()
         ecopy(c).wait_send()
 
-        @pl.when(a + 1 < rows)
+        @pl.when(more)
         def _():
             scopy(c).wait_send()
 
-    @pl.when(first)
+    @pl.when(first | early_pair)
     def _():
         kvside(0).wait_send()
 
-    for d in range(rows):
-        @pl.when((a - d >= 0) & (a + 1 < rows))
-        def _():
-            kvhop(d).wait_send()
-
-        if d > 0:
-            @pl.when(a - d >= 0)
-            def _():
-                kvside(d).wait_send()
+    @pl.when(more)
+    def _():
+        kvhop(0, b).wait_send()
+
+    @pl.when(early_pair)
+    def _():
+        kvhop(0, 1 - b).wait_send()
+
+    def settle(d, _):
+        @pl.when(a - d >= crossing)
+        def _():
+            kvside(d).wait_send()
+
+            @pl.when(more)
+            def _():
+                kvhop(d, b).wait_send()
+
+        @pl.when((a - d < crossing) & more)
+        def _():
+            for e in range(2):
+                kvhop(d, e).wait_send()
+
+        return 0
+
+    lax.fori_loop(1, a + 1, settle, 0)
 
 
 def specs(count):
@@ -347,7 +383,7 @@
             pltpu.VMEM((KVH, big, T), F32),
             pltpu.VMEM((KVH, big, DH), F32),
             sem((CHUNKS,)), sem((CHUNKS,)), sem((2,)), sem((CHUNKS,)), sem((CHUNKS,)),
-            sem((CHUNKS,)), sem((CHUNKS,)), sem((rows,)), sem((n,)), sem((rows,)),
+            sem((CHUNKS,)), sem((CHUNKS,)), sem((rows, 2)), sem((n,)), sem((rows,)),
         ],
         compiler_params=pltpu.CompilerParams(
             collective_id=0, has_side_effects=True, vmem_limit_bytes=VMEM_LIMIT

time: 39.6 us -> 66.5 us (1.68)
  the two profiles are of different devices: /device:TPU:28 before, /device:TPU:26 now
where the time goes in v4:
time: 66.5 us; the launch traced here: 65.3 us
  Pallas kernels  61.8 us (93%)
  local copies, waits for them, and re-layouts  2.87 us (4%)
    pallas_call x1, Pallas kernels, per_device(): pl.pallas_call(functools.partial(kernel, n), out_shape=(jax.ShapeDtypeStr...  61.8 us
    unnamed x4, local copies, waits for them, and re-layouts  2.87 us

profile of v4, /device:TPU:26, one launch (start us, length us, event | category | flops | bytes accessed | tf_op | source)
XLA Modules:
  0.0 65.3 jit_solution(12749238990571774705)
XLA Ops:
  0.6 61.8 %mix_and_attend.1 = (bf16[128,2560]{1,0:T(8,128)(2,1)}, bf16[128,2560]{1,0:T(8,128)(2,1)}) custom-call(bf16[128,2560]{1,0:T(8,128)(2,1)} %x_ref.1, bf16[128,128]{1,0:T(8,128)(2,1)} %in_ref.1, bf16[128,128]{1,0:T(8,128)(2,1)} %out_ref.1, f32[40,128]{1,0:T(8,128)} %bitcast.5, bf16[128,2560]{1,0:T(8,128)(2,1)} %q_ref.1, bf16[320,128]{1,0:T(8,128)(2,1)} %bitcast.3, ...), custom_call_target="tpu_custom_call" | custom-call | tf_op jit(solution)/shard_map/mix_and_attend/pallas_call | solution.py:365
  62.4 0.0 copy-start
  62.4 2.0 %copy.11 = bf16[128,2560]{1,0:T(8,128)(2,1)} copy(bf16[128,2560]{1,0:T(8,128)(2,1)} %get-tuple-element.4) | data formatting | bytes 1310720
  64.5 0.0 copy-done
  64.5 0.8 %copy.12 = bf16[128,2560]{1,0:T(8,128)(2,1)} copy(bf16[128,2560]{1,0:T(8,128)(2,1)S(1)} %copy-done) | data formatting | bytes 1310720
Async XLA Ops:
  62.4 2.0 %copy-start = (bf16[128,2560]{1,0:T(8,128)(2,1)S(1)}, bf16[128,2560]{1,0:T(8,128)(2,1)}, u32[]{:S(2)}) copy-start(bf16[128,2560]{1,0:T(8,128)(2,1)} %get-tuple-element.5) | copy-start | bytes 1966084

commit v5 on v4

--- a/solution.py
+++ b/solution.py
@@ -55,7 +55,7 @@
     ahead = (dp, lax.rem(a + 1, rows) * 2 + b)
     behind = (dp, lax.rem(a + rows - 1, rows) * 2 + b)
     first = b == 0
-    crossing = rows // 2
+    crossing = max(1, rows // 4)
     early_pair = a < crossing
     more = a + 1 < rows
 
@@ -104,6 +104,10 @@
     @pl.when(more)
     def _():
         kvhop(0, b).start()
+
+    @pl.when(first | early_pair)
+    def _():
+        kvside(0).start()
 
     lower = iota((T, T), 0) >= iota((T, T), 1)
     triu = jnp.where(iota((T, T), 0) <= iota((T, T), 1), 1.0, 0.0).astype(F32)
@@ -140,33 +144,30 @@
                 )
         usend[c] = u[1 - b, c].astype(BF)
         ucopy(c).start()
-        if c == 0:
-            @pl.when(first | early_pair)
-            def _():
-                kvside(0).start()
 
     @pl.when(first & jnp.logical_not(early_pair))
     def _():
         kvall[me + 1] = jnp.zeros((KV_ROWS, T), BF)
 
     def hand_on(d):
-        @pl.when(a - d >= crossing)
+        @pl.when(a - d >= 0)
         def _():
             kvarrive(me - 2 * d)
-            kvside(d).start()
 
             @pl.when(more)
             def _():
                 kvhop(d, b).start()
 
-        @pl.when((a - d >= 0) & (a - d < crossing))
-        def _():
-            for e in range(2):
-                kvarrive((a - d) * 2 + e)
-
-                @pl.when(more)
-                def _():
-                    kvhop(d, e).start()
+        @pl.when(a - d >= crossing)
+        def _():
+            kvside(d).start()
+
+    def hand_other(d):
+        kvarrive((a - d) * 2 + 1 - b)
+
+        @pl.when((a - d < crossing) & more)
+        def _():
+            kvhop(d, 1 - b).start()
 
     def chain():
         fcopy().wait_recv()
@@ -266,31 +267,23 @@
 
     hand_on(1)
 
+    @pl.when((b == 1) | early_pair)
+    def _():
+        hand_other(0)
+
     @pl.when(a == 0)
     def _():
         chain()
-
-    @pl.when((b == 1) | early_pair)
-    def _():
-        kvarrive(a * 2 + 1 - b)
-
-    @pl.when(early_pair)
-    def _():
-        kvhop(0, 1 - b).start()
 
     attend(a, True)
 
     def step(d, _):
         hand_on(d + 1)
+        hand_other(d)
 
         @pl.when(a == d)
         def _():
             chain()
-
-
-        @pl.when(a - d >= crossing)
-        def _():
-            kvarrive((a - d) * 2 + 1 - b)
 
         attend(a - d, False)
         return 0
@@ -325,31 +318,22 @@
     def _():
         kvside(0).wait_send()
 
-    @pl.when(more)
-    def _():
-        kvhop(0, b).wait_send()
-
-    @pl.when(early_pair)
-    def _():
-        kvhop(0, 1 - b).wait_send()
-
     def settle(d, _):
-        @pl.when(a - d >= crossing)
+        @pl.when((a - d >= crossing) & (d > 0))
         def _():
             kvside(d).wait_send()
 
-            @pl.when(more)
-            def _():
-                kvhop(d, b).wait_send()
+        @pl.when(more)
+        def _():
+            kvhop(d, b).wait_send()
 
         @pl.when((a - d < crossing) & more)
         def _():
-            for e in range(2):
-                kvhop(d, e).wait_send()
+            kvhop(d, 1 - b).wait_send()
 
         return 0
 
-    lax.fori_loop(1, a + 1, settle, 0)
+    lax.fori_loop(0, a + 1, settle, 0)
 
 
 def specs(count):

time: 66.5 us -> 41.5 us (0.62); the launches traced: 65.3 us -> 41.3 us
  Pallas kernels: 61.8 us -> 37.8 us
    pallas_call x1, Pallas kernels: 61.8 us -> 37.8 us  [per_device(): pl.pallas_call(functools.partial(kernel, n), out_shape=(jax.ShapeDtypeStr...]
where the time goes in v5:
time: 41.5 us; the launch traced here: 41.3 us
  Pallas kernels  37.8 us (91%)
  local copies, waits for them, and re-layouts  2.87 us (7%)
  between operations  0.65 us (2%)
    pallas_call x1, Pallas kernels, per_device(): pl.pallas_call(functools.partial(kernel, n), out_shape=(jax.ShapeDtypeStr...  37.8 us
    unnamed x4, local copies, waits for them, and re-layouts  2.87 us

profile of v5, /device:TPU:26, one launch (start us, length us, event | category | flops | bytes accessed | tf_op | source)
XLA Modules:
  0.0 41.3 jit_solution(6960883864129695644)
XLA Ops:
  0.6 37.8 %mix_and_attend.1 = (bf16[128,2560]{1,0:T(8,128)(2,1)}, bf16[128,2560]{1,0:T(8,128)(2,1)}) custom-call(bf16[128,2560]{1,0:T(8,128)(2,1)} %x_ref.1, bf16[128,128]{1,0:T(8,128)(2,1)} %in_ref.1, bf16[128,128]{1,0:T(8,128)(2,1)} %out_ref.1, f32[40,128]{1,0:T(8,128)} %bitcast.5, bf16[128,2560]{1,0:T(8,128)(2,1)} %q_ref.1, bf16[320,128]{1,0:T(8,128)(2,1)} %bitcast.3, ...), custom_call_target="tpu_custom_call" | custom-call | tf_op jit(solution)/shard_map/mix_and_attend/pallas_call | solution.py:349
  38.4 0.0 copy-start
  38.5 2.0 %copy.11 = bf16[128,2560]{1,0:T(8,128)(2,1)} copy(bf16[128,2560]{1,0:T(8,128)(2,1)} %get-tuple-element.4) | data formatting | bytes 1310720
  40.5 0.0 copy-done
  40.5 0.8 %copy.12 = bf16[128,2560]{1,0:T(8,128)(2,1)} copy(bf16[128,2560]{1,0:T(8,128)(2,1)S(1)} %copy-done) | data formatting | bytes 1310720
Async XLA Ops:
  38.4 2.0 %copy-start = (bf16[128,2560]{1,0:T(8,128)(2,1)S(1)}, bf16[128,2560]{1,0:T(8,128)(2,1)}, u32[]{:S(2)}) copy-start(bf16[128,2560]{1,0:T(8,128)(2,1)} %get-tuple-element.5) | copy-start | bytes 1966084

commit v6 on v3

--- a/solution.py
+++ b/solution.py
@@ -198,58 +198,46 @@
         def group(g, _):
             kc = pl.ds(pl.multiple_of(g * DH, 16), DH)
             vc = pl.ds(pl.multiple_of((KVH + g) * DH, 16), DH)
-            keys = jnp.concatenate([kvall[2 * p, kc, :], kvall[2 * p + 1, kc, :]], axis=1)
+            keys = jnp.concatenate([kvall[2 * p, kc, :], kvall[2 * p + 1, kc, :]], axis=1).T
             values = jnp.concatenate([kvall[2 * p, vc, :], kvall[2 * p + 1, vc, :]], axis=1)
             if opening:
-                width = GROUP * DH
-                q = q_ref[:, pl.ds(pl.multiple_of(g * width, T), width)]
-                queries = jnp.concatenate([q[:, r * DH : (r + 1) * DH] for r in range(GROUP)], axis=0)
+                q = q_ref[:, pl.ds(pl.multiple_of(g * GROUP * DH, T), GROUP * DH)].T
+                queries = jnp.concatenate([q[r * DH : (r + 1) * DH] for r in range(GROUP)], axis=1)
                 qs[g] = queries
-                shown = iota((T, wide), 1) <= iota((T, wide), 0) + b * T
+                shown = iota((wide, wide), 0) <= (iota((wide, wide), 1) % T) + b * T
             else:
                 queries = qs[g]
                 old_top = top[g]
                 old_total = total[g]
                 old_acc = acc[g]
-            scores = dot(queries, keys)
-            peaks, totals, shrinks, expos = [], [], [], []
-            for r in range(GROUP):
-                at = slice(r * T, (r + 1) * T)
-                s = scores[at]
+            results = []
+            for r in range(GROUP // 2):
+                at = slice(r * wide, (r + 1) * wide)
+                s = dot(keys, queries[:, at])
                 if opening:
                     s = jnp.where(shown, s, MASKED)
-                peak = jnp.max(jnp.maximum(s[:, :T], s[:, T:]), axis=1, keepdims=True)
-                if opening:
-                    peak = jnp.broadcast_to(peak, (T, T))
-                else:
-                    peak = jnp.maximum(old_top[at], peak)
-                    shrinks.append(jnp.exp2((old_top[at] - peak) * EXP_SCALE))
-                peaks.append(peak)
-                e0 = jnp.exp2((s[:, :T] - peak) * EXP_SCALE)
-                e1 = jnp.exp2((s[:, T:] - peak) * EXP_SCALE)
-                totals.append(e0 + e1)
-                expos.append(jnp.concatenate([e0.astype(BF), e1.astype(BF)], axis=1))
-            summed = nt_dot(jnp.concatenate(expos, axis=0), values)
-            for r in range(GROUP):
-                at = slice(r * T, (r + 1) * T)
-                top[g, at, :] = peaks[r]
-                if opening:
-                    total[g, at, :] = totals[r]
-                    acc[g, at, :] = summed[at]
-                else:
-                    total[g, at, :] = old_total[at] * shrinks[r] + totals[r]
-                    acc[g, at, :] = old_acc[at] * shrinks[r][:, :DH] + summed[at]
+                peak = jnp.max(s, axis=0, keepdims=True)
+                if not opening:
+                    peak = jnp.maximum(old_top[:, at], peak)
+                e = jnp.exp2((s - peak) * EXP_SCALE)
+                summed = jnp.sum(e, axis=0, keepdims=True)
+                out = dot(values, e.astype(BF))
+                if not opening:
+                    shrink = jnp.exp2((old_top[:, at] - peak) * EXP_SCALE)
+                    summed = old_total[:, at] * shrink + summed
+                    out = old_acc[:, at] * shrink + out
+                results.append((peak, summed, out))
+            for r in range(GROUP // 2):
+                at = slice(r * wide, (r + 1) * wide)
+                top[g, :, at], total[g, :, at], acc[g, :, at] = results[r]
             return 0
 
         lax.fori_loop(0, KVH, group, 0)
 
     def finish(g, _):
-        width = GROUP * DH
-        outs = []
-        for r in range(GROUP):
-            at = slice(r * T, (r + 1) * T)
-            outs.append((acc[g, at, :] / jnp.sum(total[g, at, :], axis=1, keepdims=True)).astype(BF))
-        att_ref[:, pl.ds(pl.multiple_of(g * width, T), width)] = jnp.concatenate(outs, axis=1)
+        out = acc[g] / total[g]
+        tall = jnp.concatenate([out[:, r * T : (r + 1) * T] for r in range(GROUP)], axis=0)
+        att_ref[:, pl.ds(pl.multiple_of(g * GROUP * DH, T), GROUP * DH)] = tall.T.astype(BF)
         return 0
 
     hand_on(1)
@@ -342,10 +330,10 @@
             pltpu.VMEM((T, T), F32),
             chunked, chunked, pltpu.VMEM((1, HALF), F32), chunked, chunked, chunked,
             pltpu.VMEM((2, CHUNKS, N, CW), BF),
-            pltpu.VMEM((KVH, big, DH), BF),
-            pltpu.VMEM((KVH, big, T), F32),
-            pltpu.VMEM((KVH, big, T), F32),
-            pltpu.VMEM((KVH, big, DH), F32),
+            pltpu.VMEM((KVH, DH, big), BF),
+            pltpu.VMEM((KVH, 1, big), F32),
+            pltpu.VMEM((KVH, 1, big), F32),
+            pltpu.VMEM((KVH, DH, big), F32),
             sem((CHUNKS,)), sem((CHUNKS,)), sem((2,)), sem((CHUNKS,)), sem((CHUNKS,)),
             sem((CHUNKS,)), sem((CHUNKS,)), sem((rows,)), sem((n,)), sem((rows,)),
         ],

time: 39.6 us -> 43.1 us (1.088)
  the two profiles are of different devices: /device:TPU:28 before, /device:TPU:26 now
where the time goes in v6:
time: 43.1 us; the launch traced here: 42.9 us
  Pallas kernels  39.4 us (91%)
  local copies, waits for them, and re-layouts  2.87 us (7%)
  between operations  0.65 us (2%)
    pallas_call x1, Pallas kernels, per_device(): pl.pallas_call(functools.partial(kernel, n), out_shape=(jax.ShapeDtypeStr...  39.4 us
    unnamed x4, local copies, waits for them, and re-layouts  2.87 us

profile of v6, /device:TPU:26, one launch (start us, length us, event | category | flops | bytes accessed | tf_op | source)
XLA Modules:
  0.0 42.9 jit_solution(8582195604599734832)
XLA Ops:
  0.6 39.4 %mix_and_attend.1 = (bf16[128,2560]{1,0:T(8,128)(2,1)}, bf16[128,2560]{1,0:T(8,128)(2,1)}) custom-call(bf16[128,2560]{1,0:T(8,128)(2,1)} %x_ref.1, bf16[128,128]{1,0:T(8,128)(2,1)} %in_ref.1, bf16[128,128]{1,0:T(8,128)(2,1)} %out_ref.1, f32[40,128]{1,0:T(8,128)} %bitcast.5, bf16[128,2560]{1,0:T(8,128)(2,1)} %q_ref.1, bf16[320,128]{1,0:T(8,128)(2,1)} %bitcast.3, ...), custom_call_target="tpu_custom_call" | custom-call | tf_op jit(solution)/shard_map/mix_and_attend/pallas_call | solution.py:317
  40.0 0.0 copy-start
  40.1 2.0 %copy.11 = bf16[128,2560]{1,0:T(8,128)(2,1)} copy(bf16[128,2560]{1,0:T(8,128)(2,1)} %get-tuple-element.4) | data formatting | bytes 1310720
  42.1 0.0 copy-done
  42.1 0.8 %copy.12 = bf16[128,2560]{1,0:T(8,128)(2,1)} copy(bf16[128,2560]{1,0:T(8,128)(2,1)S(1)} %copy-done) | data formatting | bytes 1310720
Async XLA Ops:
  40.0 2.0 %copy-start = (bf16[128,2560]{1,0:T(8,128)(2,1)S(1)}, bf16[128,2560]{1,0:T(8,128)(2,1)}, u32[]{:S(2)}) copy-start(bf16[128,2560]{1,0:T(8,128)(2,1)} %get-tuple-element.5) | copy-start | bytes 1966084

commit v7 on v3

--- a/solution.py
+++ b/solution.py
@@ -254,7 +254,7 @@
 
     hand_on(1)
 
-    @pl.when(a == 0)
+    @pl.when(a <= 1)
     def _():
         chain()
 
@@ -267,7 +267,7 @@
     def step(d, _):
         hand_on(d + 1)
 
-        @pl.when(a == d)
+        @pl.when((a >= 2) & (d == jnp.where(a == 2, 1, jnp.minimum(a, 3))))
         def _():
             chain()
 
@@ -316,6 +316,18 @@
                 kvside(d).wait_send()
 
 
+def deliver_kernel(mix_ref, att_ref, mix_out, att_out, done):
+    copies = []
+    for k, (src, dst) in enumerate(((mix_ref, mix_out), (att_ref, att_out))):
+        for half in range(2):
+            at = pl.ds(half * (T // 2), T // 2)
+            copies.append(pltpu.make_async_copy(src.at[at], dst.at[at], done.at[2 * k + half]))
+    for copy in copies:
+        copy.start()
+    for copy in copies:
+        copy.wait()
+
+
 def specs(count):
     return [pl.BlockSpec(memory_space=pltpu.VMEM)] * count
 
@@ -326,7 +338,7 @@
     sem = pltpu.SemaphoreType.DMA
     chunked = pltpu.VMEM((CHUNKS, N, CW), BF)
     big = GROUP * T
-    return pl.pallas_call(
+    mixed, attended = pl.pallas_call(
         functools.partial(kernel, n),
         out_shape=(
             jax.ShapeDtypeStruct((T, width), BF),
@@ -354,6 +366,17 @@
         ),
         name="mix_and_attend",
     )(mixer_input, input_map, output_map, log_decay.T, query_rows, key_rows.T, value_rows.T)
+    return pl.pallas_call(
+        deliver_kernel,
+        out_shape=(
+            jax.ShapeDtypeStruct((T, width), BF),
+            jax.ShapeDtypeStruct((T, QH * DH), BF),
+        ),
+        in_specs=[pl.BlockSpec(memory_space=pl.ANY)] * 2,
+        out_specs=[pl.BlockSpec(memory_space=pl.ANY)] * 2,
+        scratch_shapes=[sem((4,))],
+        name="deliver",
+    )(mixed, attended)
 
 
 def solution(mesh):

time: 39.6 us -> 77.6 us (1.96)
  the two profiles are of different devices: /device:TPU:28 before, /device:TPU:26 now
where the time goes in v7:
time: 77.6 us; the launch traced here: 76.1 us
  Pallas kernels  75.4 us (97%)
    pallas_call x1, Pallas kernels, per_device(): pl.pallas_call(deliver_kernel, out_shape=(jax.ShapeDtypeStruct((T, width)...  40.8 us
    pallas_call x1, Pallas kernels, per_device(): pl.pallas_call(functools.partial(kernel, n), out_shape=(jax.ShapeDtypeStr...  34.6 us

profile of v7, /device:TPU:26, one launch (start us, length us, event | category | flops | bytes accessed | tf_op | source)
XLA Modules:
  0.0 76.1 jit_solution(2919306315460531094)
XLA Ops:
  0.6 34.6 %mix_and_attend.1 = (bf16[128,2560]{1,0:T(8,128)(2,1)}, bf16[128,2560]{1,0:T(8,128)(2,1)}) custom-call(bf16[128,2560]{1,0:T(8,128)(2,1)} %x_ref.1, bf16[128,128]{1,0:T(8,128)(2,1)} %in_ref.1, bf16[128,128]{1,0:T(8,128)(2,1)} %out_ref.1, f32[40,128]{1,0:T(8,128)} %bitcast.5, bf16[128,2560]{1,0:T(8,128)(2,1)} %q_ref.1, bf16[320,128]{1,0:T(8,128)(2,1)} %bitcast.3, ...), custom_call_target="tpu_custom_call" | custom-call | tf_op jit(solution)/shard_map/mix_and_attend/pallas_call | solution.py:341
  35.2 40.8 %deliver.1 = (bf16[128,2560]{1,0:T(8,128)(2,1)}, bf16[128,2560]{1,0:T(8,128)(2,1)}) custom-call(bf16[128,2560]{1,0:T(8,128)(2,1)} %get-tuple-element.4.mix_ref, bf16[128,2560]{1,0:T(8,128)(2,1)} %get-tuple-element.5.att_ref), custom_call_target="tpu_custom_call" | custom-call | tf_op jit(solution)/shard_map/deliver/pallas_call | solution.py:369

commit v8 on v7

--- a/solution.py
+++ b/solution.py
@@ -18,6 +18,7 @@
 GROUP = QH // KVH
 KV_ROWS = 2 * KVH * DH
 CHUNKS = 5
+NEAR = 3
 CW = 256
 PAIRS = MIXER_HEADS // 2
 HALF = MIXER_HEADS * P_SIZE // 2
@@ -45,7 +46,7 @@
     n, x_ref, in_ref, out_ref, ld_ref, q_ref, k_ref, v_ref, mix_ref, att_ref,
     kvall, u, f, inner, ecum_ref, usend, urecv, frecv, sin, sout, entsend, ent,
     qs, top, total, acc,
-    us_sem, ur_sem, f_sem, ss_sem, sr_sem, es_sem, er_sem, kvs_sem, kvr_sem, px_sem,
+    us_sem, ur_sem, f_sem, ss_sem, sr_sem, es_sem, er_sem, kvs_sem, kvr_sem, px_sem, far_sem,
 ):
     dp = lax.axis_index("dp")
     me = lax.axis_index("ctx")
@@ -88,19 +89,35 @@
             src_ref=kvall.at[block], dst_ref=kvall.at[block], send_sem=px_sem.at[d],
             recv_sem=kvr_sem.at[block], device_id=partner, device_id_type=MESH)
 
+    def kvfar(d):
+        return pltpu.make_async_remote_copy(
+            src_ref=kvall.at[me], dst_ref=kvall.at[me], send_sem=far_sem.at[d],
+            recv_sem=kvr_sem.at[me], device_id=(dp, lax.rem(a + d, rows) * 2 + 1 - b),
+            device_id_type=MESH)
+
     def kvarrive(block):
         pltpu.make_async_copy(kvall.at[block], kvall.at[block], kvr_sem.at[block]).wait()
 
     barrier = pltpu.get_barrier_semaphore()
-    for device in (partner, ahead, behind):
+    across = [(dp, lax.rem(a + d, rows) * 2 + 1 - b) for d in range(1, rows)] if rows > NEAR else []
+    for device in [partner, ahead, behind] + across:
         pl.semaphore_signal(barrier, inc=1, device_id=device, device_id_type=MESH)
     kvall[me, : KVH * DH, :] = k_ref[...]
     kvall[me, KVH * DH :, :] = v_ref[...]
-    pl.semaphore_wait(barrier, 3)
+    pl.semaphore_wait(barrier, 3 + len(across))
 
     @pl.when(a + 1 < rows)
     def _():
         kvhop(0).start()
+
+    for d in range(NEAR, rows):
+        @pl.when(a + d < rows)
+        def _():
+            kvfar(d).start()
+
+    @pl.when(first & (a >= 2))
+    def _():
+        kvside(0).start()
 
     lower = iota((T, T), 0) >= iota((T, T), 1)
     triu = jnp.where(iota((T, T), 0) <= iota((T, T), 1), 1.0, 0.0).astype(F32)
@@ -138,7 +155,7 @@
         usend[c] = u[1 - b, c].astype(BF)
         ucopy(c).start()
         if c == 0:
-            @pl.when(first)
+            @pl.when(first & (a < 2))
             def _():
                 kvside(0).start()
 
@@ -150,7 +167,10 @@
         @pl.when(a - d >= 0)
         def _():
             kvarrive(me - 2 * d)
-            kvside(d).start()
+
+            @pl.when(d < NEAR)
+            def _():
+                kvside(d).start()
 
             @pl.when(a + 1 < rows)
             def _():
@@ -310,22 +330,20 @@
         def _():
             kvhop(d).wait_send()
 
-        if d > 0:
+        if 0 < d < NEAR:
             @pl.when(a - d >= 0)
             def _():
                 kvside(d).wait_send()
 
-
-def deliver_kernel(mix_ref, att_ref, mix_out, att_out, done):
-    copies = []
-    for k, (src, dst) in enumerate(((mix_ref, mix_out), (att_ref, att_out))):
-        for half in range(2):
-            at = pl.ds(half * (T // 2), T // 2)
-            copies.append(pltpu.make_async_copy(src.at[at], dst.at[at], done.at[2 * k + half]))
-    for copy in copies:
-        copy.start()
-    for copy in copies:
-        copy.wait()
+        if d >= NEAR:
+            @pl.when(a + d < rows)
+            def _():
+                kvfar(d).wait_send()
+
+
+def deliver_kernel(mix_ref, att_ref, mix_out, att_out):
+    mix_out[...] = mix_ref[...]
+    att_out[...] = att_ref[...]
 
 
 def specs(count):
@@ -359,7 +377,7 @@
             pltpu.VMEM((KVH, big, T), F32),
             pltpu.VMEM((KVH, big, DH), F32),
             sem((CHUNKS,)), sem((CHUNKS,)), sem((2,)), sem((CHUNKS,)), sem((CHUNKS,)),
-            sem((CHUNKS,)), sem((CHUNKS,)), sem((rows,)), sem((n,)), sem((rows,)),
+            sem((CHUNKS,)), sem((CHUNKS,)), sem((rows,)), sem((n,)), sem((NEAR,)), sem((rows,)),
         ],
         compiler_params=pltpu.CompilerParams(
             collective_id=0, has_side_effects=True, vmem_limit_bytes=VMEM_LIMIT
@@ -372,9 +390,8 @@
             jax.ShapeDtypeStruct((T, width), BF),
             jax.ShapeDtypeStruct((T, QH * DH), BF),
         ),
-        in_specs=[pl.BlockSpec(memory_space=pl.ANY)] * 2,
-        out_specs=[pl.BlockSpec(memory_space=pl.ANY)] * 2,
-        scratch_shapes=[sem((4,))],
+        in_specs=specs(2),
+        out_specs=specs(2),
         name="deliver",
     )(mixed, attended)
 

time: 77.6 us -> 40.9 us (0.53)
  the two profiles are of different devices: /device:TPU:26 before, /device:TPU:24 now
where the time goes in v8:
time: 40.9 us; the launch traced here: 40.7 us
  Pallas kernels  40.1 us (98%)
  between operations  0.64 us (2%)
    pallas_call x1, Pallas kernels, per_device(): pl.pallas_call(functools.partial(kernel, n), out_shape=(jax.ShapeDtypeStr...  37.7 us
    pallas_call x1, Pallas kernels, per_device(): pl.pallas_call(deliver_kernel, out_shape=(jax.ShapeDtypeStruct((T, width)...  2.38 us

profile of v8, /device:TPU:24, one launch (start us, length us, event | category | flops | bytes accessed | tf_op | source)
XLA Modules:
  0.0 40.7 jit_solution(6551409283098036179)
XLA Ops:
  0.6 37.7 %mix_and_attend.1 = (bf16[128,2560]{1,0:T(8,128)(2,1)}, bf16[128,2560]{1,0:T(8,128)(2,1)}) custom-call(bf16[128,2560]{1,0:T(8,128)(2,1)} %x_ref.1, bf16[128,128]{1,0:T(8,128)(2,1)} %in_ref.1, bf16[128,128]{1,0:T(8,128)(2,1)} %out_ref.1, f32[40,128]{1,0:T(8,128)} %bitcast.5, bf16[128,2560]{1,0:T(8,128)(2,1)} %q_ref.1, bf16[320,128]{1,0:T(8,128)(2,1)} %bitcast.3, ...), custom_call_target="tpu_custom_call" | custom-call | tf_op jit(solution)/shard_map/mix_and_attend/pallas_call | solution.py:359
  38.3 2.4 %deliver.1 = (bf16[128,2560]{1,0:T(8,128)(2,1)}, bf16[128,2560]{1,0:T(8,128)(2,1)}) custom-call(bf16[128,2560]{1,0:T(8,128)(2,1)} %get-tuple-element.4.mix_ref, bf16[128,2560]{1,0:T(8,128)(2,1)} %get-tuple-element.5.att_ref), custom_call_target="tpu_custom_call" | custom-call | tf_op jit(solution)/shard_map/deliver/pallas_call | solution.py:387

commit v9 on v2

--- a/solution.py
+++ b/solution.py
@@ -14,6 +14,7 @@
 QH = 32
 KVH = 4
 DH = 80
+WITH_SUM = 96
 T = 128
 GROUP = QH // KVH
 KV_ROWS = 2 * KVH * DH
@@ -44,7 +45,7 @@
 def kernel(
     n, x_ref, in_ref, out_ref, ld_ref, q_ref, k_ref, v_ref, mix_ref, att_ref,
     kvall, u, f, inner, ecum_ref, usend, urecv, frecv, sin, sout, entsend, ent,
-    qs, top, total, acc,
+    qs, top, acc,
     us_sem, ur_sem, f_sem, ss_sem, sr_sem, es_sem, er_sem, kvs_sem, kvr_sem, px_sem,
 ):
     dp = lax.axis_index("dp")
@@ -201,6 +202,7 @@
             vc = pl.ds(pl.multiple_of((KVH + g) * DH, 16), DH)
             keys = jnp.concatenate([kvall[2 * p, kc, :], kvall[2 * p + 1, kc, :]], axis=1)
             values = jnp.concatenate([kvall[2 * p, vc, :], kvall[2 * p + 1, vc, :]], axis=1)
+            values = jnp.concatenate([values, jnp.ones((WITH_SUM - DH, 2 * T), BF)], axis=0)
             if opening:
                 width = GROUP * DH
                 q = q_ref[:, pl.ds(pl.multiple_of(g * width, T), width)]
@@ -225,11 +227,9 @@
                 e = jnp.concatenate([e0.astype(BF), e1.astype(BF)], axis=1)
                 summed = nt_dot(e, values)
                 if opening:
-                    total[g, at, :] = e0 + e1
                     acc[g, at, :] = summed
                 else:
-                    total[g, at, :] = total[g, at, :] * shrink + (e0 + e1)
-                    acc[g, at, :] = acc[g, at, :] * shrink[:, :DH] + summed
+                    acc[g, at, :] = acc[g, at, :] * shrink[:, :WITH_SUM] + summed
             return 0
 
         lax.fori_loop(0, KVH, group, 0)
@@ -239,7 +239,8 @@
         outs = []
         for r in range(GROUP):
             at = slice(r * T, (r + 1) * T)
-            outs.append((acc[g, at, :] / jnp.sum(total[g, at, :], axis=1, keepdims=True)).astype(BF))
+            whole = acc[g, at, :]
+            outs.append((whole[:, :DH] / whole[:, DH : DH + 1]).astype(BF))
         att_ref[:, pl.ds(pl.multiple_of(g * width, T), width)] = jnp.concatenate(outs, axis=1)
         return 0
 
@@ -302,6 +303,11 @@
                 kvside(d).wait_send()
 
 
+def deliver_kernel(mix_ref, att_ref, mix_out, att_out):
+    mix_out[...] = mix_ref[...]
+    att_out[...] = att_ref[...]
+
+
 def specs(count):
     return [pl.BlockSpec(memory_space=pltpu.VMEM)] * count
 
@@ -312,7 +318,7 @@
     sem = pltpu.SemaphoreType.DMA
     chunked = pltpu.VMEM((CHUNKS, N, CW), BF)
     big = GROUP * T
-    return pl.pallas_call(
+    mixed, attended = pl.pallas_call(
         functools.partial(kernel, n),
         out_shape=(
             jax.ShapeDtypeStruct((T, width), BF),
@@ -330,8 +336,7 @@
             pltpu.VMEM((2, CHUNKS, N, CW), BF),
             pltpu.VMEM((KVH, big, DH), BF),
             pltpu.VMEM((KVH, big, T), F32),
-            pltpu.VMEM((KVH, big, T), F32),
-            pltpu.VMEM((KVH, big, DH), F32),
+            pltpu.VMEM((KVH, big, WITH_SUM), F32),
             sem((CHUNKS,)), sem((CHUNKS,)), sem((2,)), sem((CHUNKS,)), sem((CHUNKS,)),
             sem((CHUNKS,)), sem((CHUNKS,)), sem((rows,)), sem((n,)), sem((rows,)),
         ],
@@ -340,6 +345,16 @@
         ),
         name="mix_and_attend",
     )(mixer_input, input_map, output_map, log_decay.T, query_rows, key_rows.T, value_rows.T)
+    return pl.pallas_call(
+        deliver_kernel,
+        out_shape=(
+            jax.ShapeDtypeStruct((T, width), BF),
+            jax.ShapeDtypeStruct((T, QH * DH), BF),
+        ),
+        in_specs=specs(2),
+        out_specs=specs(2),
+        name="deliver",
+    )(mixed, attended)
 
 
 def solution(mesh):

time: 39.2 us -> 38.6 us (0.985)
  local copies, waits for them, and re-layouts: 2.87 us -> 0 us
  Pallas kernels: 35.5 us -> 37.8 us
    unnamed x4 -> x0, local copies, waits for them, and re-layouts: 2.87 us -> none
    pallas_call x0 -> x1, Pallas kernels: none -> 2.38 us  [per_device(): pl.pallas_call(deliver_kernel, out_shape=(jax.ShapeDtypeStruct((T, width)...]
where the time goes in v9:
time: 38.6 us; the launch traced here: 38.4 us
  Pallas kernels  37.8 us (98%)
  between operations  0.64 us (2%)
    pallas_call x1, Pallas kernels, per_device(): pl.pallas_call(functools.partial(kernel, n), out_shape=(jax.ShapeDtypeStr...  35.4 us
    pallas_call x1, Pallas kernels, per_device(): pl.pallas_call(deliver_kernel, out_shape=(jax.ShapeDtypeStruct((T, width)...  2.38 us

profile of v9, /device:TPU:26, one launch (start us, length us, event | category | flops | bytes accessed | tf_op | source)
XLA Modules:
  0.0 38.4 jit_solution(10778922242762113260)
XLA Ops:
  0.6 35.4 %mix_and_attend.1 = (bf16[128,2560]{1,0:T(8,128)(2,1)}, bf16[128,2560]{1,0:T(8,128)(2,1)}) custom-call(bf16[128,2560]{1,0:T(8,128)(2,1)} %x_ref.1, bf16[128,128]{1,0:T(8,128)(2,1)} %in_ref.1, bf16[128,128]{1,0:T(8,128)(2,1)} %out_ref.1, f32[40,128]{1,0:T(8,128)} %bitcast.5, bf16[128,2560]{1,0:T(8,128)(2,1)} %q_ref.1, bf16[320,128]{1,0:T(8,128)(2,1)} %bitcast.3, ...), custom_call_target="tpu_custom_call" | custom-call | tf_op jit(solution)/shard_map/mix_and_attend/pallas_call | solution.py:321
  36.0 2.4 %deliver.1 = (bf16[128,2560]{1,0:T(8,128)(2,1)}, bf16[128,2560]{1,0:T(8,128)(2,1)}) custom-call(bf16[128,2560]{1,0:T(8,128)(2,1)} %get-tuple-element.4.mix_ref, bf16[128,2560]{1,0:T(8,128)(2,1)} %get-tuple-element.5.att_ref), custom_call_target="tpu_custom_call" | custom-call | tf_op jit(solution)/shard_map/deliver/pallas_call | solution.py:348
